TPU v7x, 512 devices: a whole 4x4x16 slice. The times are simulated.
512 devices in a mesh: seq: 64 (over y, z), head: 8 (over x, core).
Axes of the slice: x: 4, y: 4, z: 16, core: 2. Of those that a mesh axis runs over, the one named last changes fastest.
Arguments:
- ssm_input: bfloat16 [65536, 4096], P('seq', 'head'), may hold values from -125 to 125
- gate_input: bfloat16 [65536, 4096], P('seq', 'head'), may hold values from -8 to 8
- write_proj: bfloat16 [65536, 128], P('seq'), may hold values from -0.1875 to 0.1875
- read_proj: bfloat16 [65536, 128], P('seq'), may hold values from -0.5 to 0.5
- decay_codes: int32 [32, 65536], P('head', 'seq'), may hold values from 1 to 131072
- decay_rate: float32 [32], P('head'), may hold values from 0.8 to 6000
- skip_gain: float32 [32], P('head'), may hold values from 0.5 to 1.5
- norm_gain: float32 [4096], P('head'), may hold values from 0.5 to 1.5
Outputs:
- mamba_out: bfloat16 [65536, 4096], P('seq', 'head')
All inputs are finite; a program needn't handle non-finite values.
Results may differ from a plain program's by a relative error of at most 0.0054.
Values sent between devices are 32-bit elements; how exact they have to be, the bound alone decides.
No kernel may reach another device: no remote copies, remote signals or barrier semaphores. Data moves between devices by JAX's collectives and lax.ppermute only.
A program may use at most 64 MiB of HBM per device.

v0:
```python
import jax
import jax.numpy as jnp
from jax import lax
from jax.sharding import PartitionSpec as P

HEADS = 32
HEAD_DIM = 128
GROUP = 256


def passed_along(block, axis, distance):
    devices = range(lax.axis_size(axis))
    route = [(i - distance, i) for i in devices if i - distance in devices]
    return lax.ppermute(block, axis, route)


def local(
    ssm_input, gate_input, write_proj, read_proj, decay_codes, decay_rate, skip_gain, norm_gain
):
    row_count, width = ssm_input.shape
    local_heads = decay_rate.shape[0]
    head_width = width // local_heads
    block_count = row_count // GROUP
    state_width = write_proj.shape[1]
    total_rows = row_count * lax.axis_size("seq")
    log_decay = -(decay_codes.astype(jnp.float32) * decay_rate[:, None]) / (8.0 * total_rows)
    cumulative = jnp.cumsum(log_decay.reshape(local_heads, block_count, GROUP), axis=2)
    x_blocks = ssm_input.reshape(block_count, GROUP, local_heads, head_width)
    write_blocks = write_proj.reshape(block_count, GROUP, state_width)
    read_blocks = read_proj.reshape(block_count, GROUP, state_width)
    positions = jnp.arange(GROUP, dtype=jnp.int32)
    causal = positions[:, None] >= positions[None, :]
    scores = jnp.einsum(
        "ktn,ksn->kts", read_blocks, write_blocks, preferred_element_type=jnp.float32
    )
    spread = cumulative[:, :, :, None] - cumulative[:, :, None, :]
    decay_mask = jnp.where(causal, jnp.exp(jnp.where(causal, spread, 0.0)), 0.0)
    mixing = (decay_mask * scores[None]).astype(jnp.bfloat16)
    inner_out = jnp.einsum("hkts,kshp->kthp", mixing, x_blocks, preferred_element_type=jnp.float32)
    block_end = cumulative[:, :, -1]
    tail = jnp.exp(block_end[:, :, None] - cumulative).transpose(1, 2, 0)
    weighted = (tail[:, :, :, None] * x_blocks.astype(jnp.float32)).astype(jnp.bfloat16)
    block_state = jnp.einsum(
        "kqn,kqhp->khnp", write_blocks, weighted, preferred_element_type=jnp.float32
    )
    block_decay = jnp.exp(block_end).T

    def advance(running, block_items):
        decay_part, state_part = block_items
        return (decay_part[:, None, None] * running + state_part, running)

    empty = jnp.zeros((local_heads, state_width, head_width), jnp.float32)
    summary, _ = lax.scan(advance, empty, (block_decay, block_state))
    device_decay = jnp.exp(jnp.sum(block_end, axis=1))

    def relay_turn(turn, pair):
        received = passed_along(pair[1], "seq", 1)
        return (received, device_decay[:, None, None] * received + summary)

    incoming, _ = lax.fori_loop(0, lax.axis_size("seq") - 1, relay_turn, (empty, summary))
    _, entering = lax.scan(advance, incoming, (block_decay, block_state))
    read_out = jnp.einsum(
        "ktn,khnp->kthp",
        read_blocks,
        entering.astype(jnp.bfloat16),
        preferred_element_type=jnp.float32,
    )
    carried = jnp.exp(cumulative).transpose(1, 2, 0)[:, :, :, None] * read_out
    ssm_out = inner_out + carried + skip_gain[None, None, :, None] * x_blocks.astype(jnp.float32)
    ssm_out = ssm_out.reshape(row_count, width)
    gated_out = ssm_out * jax.nn.silu(gate_input.astype(jnp.float32))
    row_power = lax.psum(jnp.sum(gated_out * gated_out, axis=1), "head") / (HEADS * HEAD_DIM)
    return (gated_out * lax.rsqrt(row_power[:, None] + 1e-05) * norm_gain[None, :]).astype(
        jnp.bfloat16
    )


def solution(mesh):
    placed = (
        P("seq", "head"),
        P("seq", "head"),
        P("seq", None),
        P("seq", None),
        P("head", "seq"),
        P("head"),
        P("head"),
        P("head"),
    )
    return jax.shard_map(
        local, mesh=mesh, in_specs=placed, out_specs=P("seq", "head"), check_vma=False
    )
```

profile of v0, /device:TPU:25, one launch (start us, length us, event | category | flops | bytes accessed | tf_op | source)
XLA Modules:
  0.0 796.1 jit_solution(641200525603004400)
XLA Ops:
  13.7 684.0 %while.35 = (s32[]{:T(128)}, f32[4,128,128]{2,1,0:T(8,128)}, f32[4,128,128]{2,1,0:T(8,128)S(1)}, f32[4]{0:T(128)S(1)}, f32[4,128,128]{2,1,0:T(8,128)S(1)}, /*index=5*/s32[]{:T(128)}) while((s32[]{:T(128)}, f32[4,128,128]{2,1,0:T(8,128)}, f32[4,128,128]{2,1,0:T(8,128)S(1)}, f32[4]{0:T(128)S(1)}, f32[4,128,128]{2,1,0:T(8,128)S(1)}, ...), condition=%wide.region_6.7_spmd, body=%wide.region_5.6_spmd.sunk | while | flops 131074 | bytes 2883737 | solution.py:60
  17.2 13.8 %collective-permute-done = f32[4,128,128]{2,1,0:T(8,128)S(1)} collective-permute-done((f32[4,128,128]{2,1,0:T(8,128)S(1)}, f32[4,128,128]{2,1,0:T(8,128)S(1)}, u32[]{:S(2)}, u32[]{:S(2)}) %collective-permute-start) | collective-permute-done | bytes 262176 | tf_op jit(solution)/shard_map/while/body/eval_jaxpr/ppermute | solution.py:14
  33.6 8.6 %collective-permute-done = f32[4,128,128]{2,1,0:T(8,128)S(1)} collective-permute-done((f32[4,128,128]{2,1,0:T(8,128)S(1)}, f32[4,128,128]{2,1,0:T(8,128)S(1)}, u32[]{:S(2)}, u32[]{:S(2)}) %collective-permute-start) | collective-permute-done | bytes 262176 | tf_op jit(solution)/shard_map/while/body/eval_jaxpr/ppermute | solution.py:14
  104.8 8.3 %collective-permute-done = f32[4,128,128]{2,1,0:T(8,128)S(1)} collective-permute-done((f32[4,128,128]{2,1,0:T(8,128)S(1)}, f32[4,128,128]{2,1,0:T(8,128)S(1)}, u32[]{:S(2)}, u32[]{:S(2)}) %collective-permute-start) | collective-permute-done | bytes 262176 | tf_op jit(solution)/shard_map/while/body/eval_jaxpr/ppermute | solution.py:14
  115.8 9.4 %collective-permute-done = f32[4,128,128]{2,1,0:T(8,128)S(1)} collective-permute-done((f32[4,128,128]{2,1,0:T(8,128)S(1)}, f32[4,128,128]{2,1,0:T(8,128)S(1)}, u32[]{:S(2)}, u32[]{:S(2)}) %collective-permute-start) | collective-permute-done | bytes 262176 | tf_op jit(solution)/shard_map/while/body/eval_jaxpr/ppermute | solution.py:14
  127.8 10.0 %collective-permute-done = f32[4,128,128]{2,1,0:T(8,128)S(1)} collective-permute-done((f32[4,128,128]{2,1,0:T(8,128)S(1)}, f32[4,128,128]{2,1,0:T(8,128)S(1)}, u32[]{:S(2)}, u32[]{:S(2)}) %collective-permute-start) | collective-permute-done | bytes 262176 | tf_op jit(solution)/shard_map/while/body/eval_jaxpr/ppermute | solution.py:14
  140.4 9.1 %collective-permute-done = f32[4,128,128]{2,1,0:T(8,128)S(1)} collective-permute-done((f32[4,128,128]{2,1,0:T(8,128)S(1)}, f32[4,128,128]{2,1,0:T(8,128)S(1)}, u32[]{:S(2)}, u32[]{:S(2)}) %collective-permute-start) | collective-permute-done | bytes 262176 | tf_op jit(solution)/shard_map/while/body/eval_jaxpr/ppermute | solution.py:14
  152.1 8.2 %collective-permute-done = f32[4,128,128]{2,1,0:T(8,128)S(1)} collective-permute-done((f32[4,128,128]{2,1,0:T(8,128)S(1)}, f32[4,128,128]{2,1,0:T(8,128)S(1)}, u32[]{:S(2)}, u32[]{:S(2)}) %collective-permute-start) | collective-permute-done | bytes 262176 | tf_op jit(solution)/shard_map/while/body/eval_jaxpr/ppermute | solution.py:14
  212.5 7.9 collective-permute-done
  223.0 8.9 %collective-permute-done = f32[4,128,128]{2,1,0:T(8,128)S(1)} collective-permute-done((f32[4,128,128]{2,1,0:T(8,128)S(1)}, f32[4,128,128]{2,1,0:T(8,128)S(1)}, u32[]{:S(2)}, u32[]{:S(2)}) %collective-permute-start) | collective-permute-done | bytes 262176 | tf_op jit(solution)/shard_map/while/body/eval_jaxpr/ppermute | solution.py:14
  234.6 10.3 %collective-permute-done = f32[4,128,128]{2,1,0:T(8,128)S(1)} collective-permute-done((f32[4,128,128]{2,1,0:T(8,128)S(1)}, f32[4,128,128]{2,1,0:T(8,128)S(1)}, u32[]{:S(2)}, u32[]{:S(2)}) %collective-permute-start) | collective-permute-done | bytes 262176 | tf_op jit(solution)/shard_map/while/body/eval_jaxpr/ppermute | solution.py:14
  247.5 9.6 %collective-permute-done = f32[4,128,128]{2,1,0:T(8,128)S(1)} collective-permute-done((f32[4,128,128]{2,1,0:T(8,128)S(1)}, f32[4,128,128]{2,1,0:T(8,128)S(1)}, u32[]{:S(2)}, u32[]{:S(2)}) %collective-permute-start) | collective-permute-done | bytes 262176 | tf_op jit(solution)/shard_map/while/body/eval_jaxpr/ppermute | solution.py:14
  259.7 8.6 %collective-permute-done = f32[4,128,128]{2,1,0:T(8,128)S(1)} collective-permute-done((f32[4,128,128]{2,1,0:T(8,128)S(1)}, f32[4,128,128]{2,1,0:T(8,128)S(1)}, u32[]{:S(2)}, u32[]{:S(2)}) %collective-permute-start) | collective-permute-done | bytes 262176 | tf_op jit(solution)/shard_map/while/body/eval_jaxpr/ppermute | solution.py:14
  330.9 8.3 %collective-permute-done = f32[4,128,128]{2,1,0:T(8,128)S(1)} collective-permute-done((f32[4,128,128]{2,1,0:T(8,128)S(1)}, f32[4,128,128]{2,1,0:T(8,128)S(1)}, u32[]{:S(2)}, u32[]{:S(2)}) %collective-permute-start) | collective-permute-done | bytes 262176 | tf_op jit(solution)/shard_map/while/body/eval_jaxpr/ppermute | solution.py:14
  341.8 9.4 %collective-permute-done = f32[4,128,128]{2,1,0:T(8,128)S(1)} collective-permute-done((f32[4,128,128]{2,1,0:T(8,128)S(1)}, f32[4,128,128]{2,1,0:T(8,128)S(1)}, u32[]{:S(2)}, u32[]{:S(2)}) %collective-permute-start) | collective-permute-done | bytes 262176 | tf_op jit(solution)/shard_map/while/body/eval_jaxpr/ppermute | solution.py:14
  353.8 10.0 %collective-permute-done = f32[4,128,128]{2,1,0:T(8,128)S(1)} collective-permute-done((f32[4,128,128]{2,1,0:T(8,128)S(1)}, f32[4,128,128]{2,1,0:T(8,128)S(1)}, u32[]{:S(2)}, u32[]{:S(2)}) %collective-permute-start) | collective-permute-done | bytes 262176 | tf_op jit(solution)/shard_map/while/body/eval_jaxpr/ppermute | solution.py:14
  366.5 9.1 %collective-permute-done = f32[4,128,128]{2,1,0:T(8,128)S(1)} collective-permute-done((f32[4,128,128]{2,1,0:T(8,128)S(1)}, f32[4,128,128]{2,1,0:T(8,128)S(1)}, u32[]{:S(2)}, u32[]{:S(2)}) %collective-permute-start) | collective-permute-done | bytes 262176 | tf_op jit(solution)/shard_map/while/body/eval_jaxpr/ppermute | solution.py:14
  378.2 8.2 %collective-permute-done = f32[4,128,128]{2,1,0:T(8,128)S(1)} collective-permute-done((f32[4,128,128]{2,1,0:T(8,128)S(1)}, f32[4,128,128]{2,1,0:T(8,128)S(1)}, u32[]{:S(2)}, u32[]{:S(2)}) %collective-permute-start) | collective-permute-done | bytes 262176 | tf_op jit(solution)/shard_map/while/body/eval_jaxpr/ppermute | solution.py:14
  449.0 8.9 %collective-permute-done = f32[4,128,128]{2,1,0:T(8,128)S(1)} collective-permute-done((f32[4,128,128]{2,1,0:T(8,128)S(1)}, f32[4,128,128]{2,1,0:T(8,128)S(1)}, u32[]{:S(2)}, u32[]{:S(2)}) %collective-permute-start) | collective-permute-done | bytes 262176 | tf_op jit(solution)/shard_map/while/body/eval_jaxpr/ppermute | solution.py:14
  460.6 10.3 %collective-permute-done = f32[4,128,128]{2,1,0:T(8,128)S(1)} collective-permute-done((f32[4,128,128]{2,1,0:T(8,128)S(1)}, f32[4,128,128]{2,1,0:T(8,128)S(1)}, u32[]{:S(2)}, u32[]{:S(2)}) %collective-permute-start) | collective-permute-done | bytes 262176 | tf_op jit(solution)/shard_map/while/body/eval_jaxpr/ppermute | solution.py:14
  473.6 9.6 %collective-permute-done = f32[4,128,128]{2,1,0:T(8,128)S(1)} collective-permute-done((f32[4,128,128]{2,1,0:T(8,128)S(1)}, f32[4,128,128]{2,1,0:T(8,128)S(1)}, u32[]{:S(2)}, u32[]{:S(2)}) %collective-permute-start) | collective-permute-done | bytes 262176 | tf_op jit(solution)/shard_map/while/body/eval_jaxpr/ppermute | solution.py:14
  485.7 8.6 %collective-permute-done = f32[4,128,128]{2,1,0:T(8,128)S(1)} collective-permute-done((f32[4,128,128]{2,1,0:T(8,128)S(1)}, f32[4,128,128]{2,1,0:T(8,128)S(1)}, u32[]{:S(2)}, u32[]{:S(2)}) %collective-permute-start) | collective-permute-done | bytes 262176 | tf_op jit(solution)/shard_map/while/body/eval_jaxpr/ppermute | solution.py:14
  556.9 8.3 %collective-permute-done = f32[4,128,128]{2,1,0:T(8,128)S(1)} collective-permute-done((f32[4,128,128]{2,1,0:T(8,128)S(1)}, f32[4,128,128]{2,1,0:T(8,128)S(1)}, u32[]{:S(2)}, u32[]{:S(2)}) %collective-permute-start) | collective-permute-done | bytes 262176 | tf_op jit(solution)/shard_map/while/body/eval_jaxpr/ppermute | solution.py:14
  567.9 9.4 %collective-permute-done = f32[4,128,128]{2,1,0:T(8,128)S(1)} collective-permute-done((f32[4,128,128]{2,1,0:T(8,128)S(1)}, f32[4,128,128]{2,1,0:T(8,128)S(1)}, u32[]{:S(2)}, u32[]{:S(2)}) %collective-permute-start) | collective-permute-done | bytes 262176 | tf_op jit(solution)/shard_map/while/body/eval_jaxpr/ppermute | solution.py:14
  579.9 10.0 %collective-permute-done = f32[4,128,128]{2,1,0:T(8,128)S(1)} collective-permute-done((f32[4,128,128]{2,1,0:T(8,128)S(1)}, f32[4,128,128]{2,1,0:T(8,128)S(1)}, u32[]{:S(2)}, u32[]{:S(2)}) %collective-permute-start) | collective-permute-done | bytes 262176 | tf_op jit(solution)/shard_map/while/body/eval_jaxpr/ppermute | solution.py:14
  592.5 9.1 %collective-permute-done = f32[4,128,128]{2,1,0:T(8,128)S(1)} collective-permute-done((f32[4,128,128]{2,1,0:T(8,128)S(1)}, f32[4,128,128]{2,1,0:T(8,128)S(1)}, u32[]{:S(2)}, u32[]{:S(2)}) %collective-permute-start) | collective-permute-done | bytes 262176 | tf_op jit(solution)/shard_map/while/body/eval_jaxpr/ppermute | solution.py:14
  604.2 8.2 %collective-permute-done = f32[4,128,128]{2,1,0:T(8,128)S(1)} collective-permute-done((f32[4,128,128]{2,1,0:T(8,128)S(1)}, f32[4,128,128]{2,1,0:T(8,128)S(1)}, u32[]{:S(2)}, u32[]{:S(2)}) %collective-permute-start) | collective-permute-done | bytes 262176 | tf_op jit(solution)/shard_map/while/body/eval_jaxpr/ppermute | solution.py:14
  664.6 7.9 collective-permute-done
  675.1 8.9 %collective-permute-done = f32[4,128,128]{2,1,0:T(8,128)S(1)} collective-permute-done((f32[4,128,128]{2,1,0:T(8,128)S(1)}, f32[4,128,128]{2,1,0:T(8,128)S(1)}, u32[]{:S(2)}, u32[]{:S(2)}) %collective-permute-start) | collective-permute-done | bytes 262176 | tf_op jit(solution)/shard_map/while/body/eval_jaxpr/ppermute | solution.py:14
  686.7 10.3 %collective-permute-done = f32[4,128,128]{2,1,0:T(8,128)S(1)} collective-permute-done((f32[4,128,128]{2,1,0:T(8,128)S(1)}, f32[4,128,128]{2,1,0:T(8,128)S(1)}, u32[]{:S(2)}, u32[]{:S(2)}) %collective-permute-start) | collective-permute-done | bytes 262176 | tf_op jit(solution)/shard_map/while/body/eval_jaxpr/ppermute | solution.py:14
  697.7 13.5 %while.36 = (s32[]{:T(128)}, f32[4,128,128]{2,1,0:T(8,128)}, bf16[4,4,128,128]{3,2,1,0:T(8,128)(2,1)}, f32[4,4]{1,0:T(4,128)S(1)}, f32[4,4,128,128]{3,2,1,0:T(8,128)S(1)}, /*index=5*/s32[]{:T(128)}) while((s32[]{:T(128)}, f32[4,128,128]{2,1,0:T(8,128)}, bf16[4,4,128,128]{3,2,1,0:T(8,128)(2,1)}, f32[4,4]{1,0:T(4,128)S(1)}, ...), condition=%wide.region_8.9_spmd, body=%wide.region_7.8_spmd.sunk | while | flops 131074 | bytes 1310857 | solution.py:61
  715.8 78.6 %psum.7 = f32[1024]{0:T(1024)S(1)} all-reduce(f32[1024]{0:T(1024)S(1)} %multiply_reduce_fusion), channel_id=1, replica_groups=mesh['seq'=64,'head'=8] {'head'}, use_global_device_ids=true, to_apply=%region_10.11 | all-reduce | flops 1024 | bytes 8192 | tf_op jit(solution)/shard_map/psum | solution.py:72
  (351 shorter events, 449.6 us)
Async XLA Ops:
  13.7 17.3 %collective-permute-start = (f32[4,128,128]{2,1,0:T(8,128)S(1)}, f32[4,128,128]{2,1,0:T(8,128)S(1)}, u32[]{:S(2)}, u32[]{:S(2)}) collective-permute-start(f32[4,128,128]{2,1,0:T(8,128)S(1)} %get-tuple-element.260), channel_id=1, source_target_pairs={{0,8},{8,16},{16,24},{24,32},{32,40},{40,48},{48,56},{56,64},{64,7... | collective-permute-start | bytes 786440 | tf_op jit(solution)/shard_map/while/body/eval_jaxpr/ppermute | solution.py:14
  31.7 10.6 %collective-permute-start = (f32[4,128,128]{2,1,0:T(8,128)S(1)}, f32[4,128,128]{2,1,0:T(8,128)S(1)}, u32[]{:S(2)}, u32[]{:S(2)}) collective-permute-start(f32[4,128,128]{2,1,0:T(8,128)S(1)} %get-tuple-element.260), channel_id=1, source_target_pairs={{0,8},{8,16},{16,24},{24,32},{32,40},{40,48},{48,56},{56,64},{64,7... | collective-permute-start | bytes 786440 | tf_op jit(solution)/shard_map/while/body/eval_jaxpr/ppermute | solution.py:14
  43.0 9.6 %collective-permute-start = (f32[4,128,128]{2,1,0:T(8,128)S(1)}, f32[4,128,128]{2,1,0:T(8,128)S(1)}, u32[]{:S(2)}, u32[]{:S(2)}) collective-permute-start(f32[4,128,128]{2,1,0:T(8,128)S(1)} %get-tuple-element.260), channel_id=1, source_target_pairs={{0,8},{8,16},{16,24},{24,32},{32,40},{40,48},{48,56},{56,64},{64,7... | collective-permute-start | bytes 786440 | tf_op jit(solution)/shard_map/while/body/eval_jaxpr/ppermute | solution.py:14
  102.9 10.2 %collective-permute-start = (f32[4,128,128]{2,1,0:T(8,128)S(1)}, f32[4,128,128]{2,1,0:T(8,128)S(1)}, u32[]{:S(2)}, u32[]{:S(2)}) collective-permute-start(f32[4,128,128]{2,1,0:T(8,128)S(1)} %get-tuple-element.260), channel_id=1, source_target_pairs={{0,8},{8,16},{16,24},{24,32},{32,40},{40,48},{48,56},{56,64},{64,7... | collective-permute-start | bytes 786440 | tf_op jit(solution)/shard_map/while/body/eval_jaxpr/ppermute | solution.py:14
  113.9 11.3 %collective-permute-start = (f32[4,128,128]{2,1,0:T(8,128)S(1)}, f32[4,128,128]{2,1,0:T(8,128)S(1)}, u32[]{:S(2)}, u32[]{:S(2)}) collective-permute-start(f32[4,128,128]{2,1,0:T(8,128)S(1)} %get-tuple-element.260), channel_id=1, source_target_pairs={{0,8},{8,16},{16,24},{24,32},{32,40},{40,48},{48,56},{56,64},{64,7... | collective-permute-start | bytes 786440 | tf_op jit(solution)/shard_map/while/body/eval_jaxpr/ppermute | solution.py:14
  125.9 11.9 %collective-permute-start = (f32[4,128,128]{2,1,0:T(8,128)S(1)}, f32[4,128,128]{2,1,0:T(8,128)S(1)}, u32[]{:S(2)}, u32[]{:S(2)}) collective-permute-start(f32[4,128,128]{2,1,0:T(8,128)S(1)} %get-tuple-element.260), channel_id=1, source_target_pairs={{0,8},{8,16},{16,24},{24,32},{32,40},{40,48},{48,56},{56,64},{64,7... | collective-permute-start | bytes 786440 | tf_op jit(solution)/shard_map/while/body/eval_jaxpr/ppermute | solution.py:14
  138.5 11.0 %collective-permute-start = (f32[4,128,128]{2,1,0:T(8,128)S(1)}, f32[4,128,128]{2,1,0:T(8,128)S(1)}, u32[]{:S(2)}, u32[]{:S(2)}) collective-permute-start(f32[4,128,128]{2,1,0:T(8,128)S(1)} %get-tuple-element.260), channel_id=1, source_target_pairs={{0,8},{8,16},{16,24},{24,32},{32,40},{40,48},{48,56},{56,64},{64,7... | collective-permute-start | bytes 786440 | tf_op jit(solution)/shard_map/while/body/eval_jaxpr/ppermute | solution.py:14
  150.2 10.1 %collective-permute-start = (f32[4,128,128]{2,1,0:T(8,128)S(1)}, f32[4,128,128]{2,1,0:T(8,128)S(1)}, u32[]{:S(2)}, u32[]{:S(2)}) collective-permute-start(f32[4,128,128]{2,1,0:T(8,128)S(1)} %get-tuple-element.260), channel_id=1, source_target_pairs={{0,8},{8,16},{16,24},{24,32},{32,40},{40,48},{48,56},{56,64},{64,7... | collective-permute-start | bytes 786440 | tf_op jit(solution)/shard_map/while/body/eval_jaxpr/ppermute | solution.py:14
  210.6 9.8 %collective-permute-start = (f32[4,128,128]{2,1,0:T(8,128)S(1)}, f32[4,128,128]{2,1,0:T(8,128)S(1)}, u32[]{:S(2)}, u32[]{:S(2)}) collective-permute-start(f32[4,128,128]{2,1,0:T(8,128)S(1)} %get-tuple-element.260), channel_id=1, source_target_pairs={{0,8},{8,16},{16,24},{24,32},{32,40},{40,48},{48,56},{56,64},{64,7... | collective-permute-start | bytes 786440 | tf_op jit(solution)/shard_map/while/body/eval_jaxpr/ppermute | solution.py:14
  221.1 10.9 %collective-permute-start = (f32[4,128,128]{2,1,0:T(8,128)S(1)}, f32[4,128,128]{2,1,0:T(8,128)S(1)}, u32[]{:S(2)}, u32[]{:S(2)}) collective-permute-start(f32[4,128,128]{2,1,0:T(8,128)S(1)} %get-tuple-element.260), channel_id=1, source_target_pairs={{0,8},{8,16},{16,24},{24,32},{32,40},{40,48},{48,56},{56,64},{64,7... | collective-permute-start | bytes 786440 | tf_op jit(solution)/shard_map/while/body/eval_jaxpr/ppermute | solution.py:14
  232.6 12.2 %collective-permute-start = (f32[4,128,128]{2,1,0:T(8,128)S(1)}, f32[4,128,128]{2,1,0:T(8,128)S(1)}, u32[]{:S(2)}, u32[]{:S(2)}) collective-permute-start(f32[4,128,128]{2,1,0:T(8,128)S(1)} %get-tuple-element.260), channel_id=1, source_target_pairs={{0,8},{8,16},{16,24},{24,32},{32,40},{40,48},{48,56},{56,64},{64,7... | collective-permute-start | bytes 786440 | tf_op jit(solution)/shard_map/while/body/eval_jaxpr/ppermute | solution.py:14
  245.6 11.5 %collective-permute-start = (f32[4,128,128]{2,1,0:T(8,128)S(1)}, f32[4,128,128]{2,1,0:T(8,128)S(1)}, u32[]{:S(2)}, u32[]{:S(2)}) collective-permute-start(f32[4,128,128]{2,1,0:T(8,128)S(1)} %get-tuple-element.260), channel_id=1, source_target_pairs={{0,8},{8,16},{16,24},{24,32},{32,40},{40,48},{48,56},{56,64},{64,7... | collective-permute-start | bytes 786440 | tf_op jit(solution)/shard_map/while/body/eval_jaxpr/ppermute | solution.py:14
  257.8 10.6 %collective-permute-start = (f32[4,128,128]{2,1,0:T(8,128)S(1)}, f32[4,128,128]{2,1,0:T(8,128)S(1)}, u32[]{:S(2)}, u32[]{:S(2)}) collective-permute-start(f32[4,128,128]{2,1,0:T(8,128)S(1)} %get-tuple-element.260), channel_id=1, source_target_pairs={{0,8},{8,16},{16,24},{24,32},{32,40},{40,48},{48,56},{56,64},{64,7... | collective-permute-start | bytes 786440 | tf_op jit(solution)/shard_map/while/body/eval_jaxpr/ppermute | solution.py:14
  269.0 9.6 %collective-permute-start = (f32[4,128,128]{2,1,0:T(8,128)S(1)}, f32[4,128,128]{2,1,0:T(8,128)S(1)}, u32[]{:S(2)}, u32[]{:S(2)}) collective-permute-start(f32[4,128,128]{2,1,0:T(8,128)S(1)} %get-tuple-element.260), channel_id=1, source_target_pairs={{0,8},{8,16},{16,24},{24,32},{32,40},{40,48},{48,56},{56,64},{64,7... | collective-permute-start | bytes 786440 | tf_op jit(solution)/shard_map/while/body/eval_jaxpr/ppermute | solution.py:14
  329.0 10.2 %collective-permute-start = (f32[4,128,128]{2,1,0:T(8,128)S(1)}, f32[4,128,128]{2,1,0:T(8,128)S(1)}, u32[]{:S(2)}, u32[]{:S(2)}) collective-permute-start(f32[4,128,128]{2,1,0:T(8,128)S(1)} %get-tuple-element.260), channel_id=1, source_target_pairs={{0,8},{8,16},{16,24},{24,32},{32,40},{40,48},{48,56},{56,64},{64,7... | collective-permute-start | bytes 786440 | tf_op jit(solution)/shard_map/while/body/eval_jaxpr/ppermute | solution.py:14
  339.9 11.3 %collective-permute-start = (f32[4,128,128]{2,1,0:T(8,128)S(1)}, f32[4,128,128]{2,1,0:T(8,128)S(1)}, u32[]{:S(2)}, u32[]{:S(2)}) collective-permute-start(f32[4,128,128]{2,1,0:T(8,128)S(1)} %get-tuple-element.260), channel_id=1, source_target_pairs={{0,8},{8,16},{16,24},{24,32},{32,40},{40,48},{48,56},{56,64},{64,7... | collective-permute-start | bytes 786440 | tf_op jit(solution)/shard_map/while/body/eval_jaxpr/ppermute | solution.py:14
  351.9 11.9 %collective-permute-start = (f32[4,128,128]{2,1,0:T(8,128)S(1)}, f32[4,128,128]{2,1,0:T(8,128)S(1)}, u32[]{:S(2)}, u32[]{:S(2)}) collective-permute-start(f32[4,128,128]{2,1,0:T(8,128)S(1)} %get-tuple-element.260), channel_id=1, source_target_pairs={{0,8},{8,16},{16,24},{24,32},{32,40},{40,48},{48,56},{56,64},{64,7... | collective-permute-start | bytes 786440 | tf_op jit(solution)/shard_map/while/body/eval_jaxpr/ppermute | solution.py:14
  364.5 11.0 %collective-permute-start = (f32[4,128,128]{2,1,0:T(8,128)S(1)}, f32[4,128,128]{2,1,0:T(8,128)S(1)}, u32[]{:S(2)}, u32[]{:S(2)}) collective-permute-start(f32[4,128,128]{2,1,0:T(8,128)S(1)} %get-tuple-element.260), channel_id=1, source_target_pairs={{0,8},{8,16},{16,24},{24,32},{32,40},{40,48},{48,56},{56,64},{64,7... | collective-permute-start | bytes 786440 | tf_op jit(solution)/shard_map/while/body/eval_jaxpr/ppermute | solution.py:14
  376.3 10.1 %collective-permute-start = (f32[4,128,128]{2,1,0:T(8,128)S(1)}, f32[4,128,128]{2,1,0:T(8,128)S(1)}, u32[]{:S(2)}, u32[]{:S(2)}) collective-permute-start(f32[4,128,128]{2,1,0:T(8,128)S(1)} %get-tuple-element.260), channel_id=1, source_target_pairs={{0,8},{8,16},{16,24},{24,32},{32,40},{40,48},{48,56},{56,64},{64,7... | collective-permute-start | bytes 786440 | tf_op jit(solution)/shard_map/while/body/eval_jaxpr/ppermute | solution.py:14
  436.6 9.8 %collective-permute-start = (f32[4,128,128]{2,1,0:T(8,128)S(1)}, f32[4,128,128]{2,1,0:T(8,128)S(1)}, u32[]{:S(2)}, u32[]{:S(2)}) collective-permute-start(f32[4,128,128]{2,1,0:T(8,128)S(1)} %get-tuple-element.260), channel_id=1, source_target_pairs={{0,8},{8,16},{16,24},{24,32},{32,40},{40,48},{48,56},{56,64},{64,7... | collective-permute-start | bytes 786440 | tf_op jit(solution)/shard_map/while/body/eval_jaxpr/ppermute | solution.py:14
  447.1 10.9 %collective-permute-start = (f32[4,128,128]{2,1,0:T(8,128)S(1)}, f32[4,128,128]{2,1,0:T(8,128)S(1)}, u32[]{:S(2)}, u32[]{:S(2)}) collective-permute-start(f32[4,128,128]{2,1,0:T(8,128)S(1)} %get-tuple-element.260), channel_id=1, source_target_pairs={{0,8},{8,16},{16,24},{24,32},{32,40},{40,48},{48,56},{56,64},{64,7... | collective-permute-start | bytes 786440 | tf_op jit(solution)/shard_map/while/body/eval_jaxpr/ppermute | solution.py:14
  458.7 12.2 %collective-permute-start = (f32[4,128,128]{2,1,0:T(8,128)S(1)}, f32[4,128,128]{2,1,0:T(8,128)S(1)}, u32[]{:S(2)}, u32[]{:S(2)}) collective-permute-start(f32[4,128,128]{2,1,0:T(8,128)S(1)} %get-tuple-element.260), channel_id=1, source_target_pairs={{0,8},{8,16},{16,24},{24,32},{32,40},{40,48},{48,56},{56,64},{64,7... | collective-permute-start | bytes 786440 | tf_op jit(solution)/shard_map/while/body/eval_jaxpr/ppermute | solution.py:14
  471.6 11.5 %collective-permute-start = (f32[4,128,128]{2,1,0:T(8,128)S(1)}, f32[4,128,128]{2,1,0:T(8,128)S(1)}, u32[]{:S(2)}, u32[]{:S(2)}) collective-permute-start(f32[4,128,128]{2,1,0:T(8,128)S(1)} %get-tuple-element.260), channel_id=1, source_target_pairs={{0,8},{8,16},{16,24},{24,32},{32,40},{40,48},{48,56},{56,64},{64,7... | collective-permute-start | bytes 786440 | tf_op jit(solution)/shard_map/while/body/eval_jaxpr/ppermute | solution.py:14
  483.8 10.6 %collective-permute-start = (f32[4,128,128]{2,1,0:T(8,128)S(1)}, f32[4,128,128]{2,1,0:T(8,128)S(1)}, u32[]{:S(2)}, u32[]{:S(2)}) collective-permute-start(f32[4,128,128]{2,1,0:T(8,128)S(1)} %get-tuple-element.260), channel_id=1, source_target_pairs={{0,8},{8,16},{16,24},{24,32},{32,40},{40,48},{48,56},{56,64},{64,7... | collective-permute-start | bytes 786440 | tf_op jit(solution)/shard_map/while/body/eval_jaxpr/ppermute | solution.py:14
  555.0 10.2 %collective-permute-start = (f32[4,128,128]{2,1,0:T(8,128)S(1)}, f32[4,128,128]{2,1,0:T(8,128)S(1)}, u32[]{:S(2)}, u32[]{:S(2)}) collective-permute-start(f32[4,128,128]{2,1,0:T(8,128)S(1)} %get-tuple-element.260), channel_id=1, source_target_pairs={{0,8},{8,16},{16,24},{24,32},{32,40},{40,48},{48,56},{56,64},{64,7... | collective-permute-start | bytes 786440 | tf_op jit(solution)/shard_map/while/body/eval_jaxpr/ppermute | solution.py:14
  566.0 11.3 %collective-permute-start = (f32[4,128,128]{2,1,0:T(8,128)S(1)}, f32[4,128,128]{2,1,0:T(8,128)S(1)}, u32[]{:S(2)}, u32[]{:S(2)}) collective-permute-start(f32[4,128,128]{2,1,0:T(8,128)S(1)} %get-tuple-element.260), channel_id=1, source_target_pairs={{0,8},{8,16},{16,24},{24,32},{32,40},{40,48},{48,56},{56,64},{64,7... | collective-permute-start | bytes 786440 | tf_op jit(solution)/shard_map/while/body/eval_jaxpr/ppermute | solution.py:14
  578.0 11.9 %collective-permute-start = (f32[4,128,128]{2,1,0:T(8,128)S(1)}, f32[4,128,128]{2,1,0:T(8,128)S(1)}, u32[]{:S(2)}, u32[]{:S(2)}) collective-permute-start(f32[4,128,128]{2,1,0:T(8,128)S(1)} %get-tuple-element.260), channel_id=1, source_target_pairs={{0,8},{8,16},{16,24},{24,32},{32,40},{40,48},{48,56},{56,64},{64,7... | collective-permute-start | bytes 786440 | tf_op jit(solution)/shard_map/while/body/eval_jaxpr/ppermute | solution.py:14
  590.6 11.0 %collective-permute-start = (f32[4,128,128]{2,1,0:T(8,128)S(1)}, f32[4,128,128]{2,1,0:T(8,128)S(1)}, u32[]{:S(2)}, u32[]{:S(2)}) collective-permute-start(f32[4,128,128]{2,1,0:T(8,128)S(1)} %get-tuple-element.260), channel_id=1, source_target_pairs={{0,8},{8,16},{16,24},{24,32},{32,40},{40,48},{48,56},{56,64},{64,7... | collective-permute-start | bytes 786440 | tf_op jit(solution)/shard_map/while/body/eval_jaxpr/ppermute | solution.py:14
  602.3 10.1 %collective-permute-start = (f32[4,128,128]{2,1,0:T(8,128)S(1)}, f32[4,128,128]{2,1,0:T(8,128)S(1)}, u32[]{:S(2)}, u32[]{:S(2)}) collective-permute-start(f32[4,128,128]{2,1,0:T(8,128)S(1)} %get-tuple-element.260), channel_id=1, source_target_pairs={{0,8},{8,16},{16,24},{24,32},{32,40},{40,48},{48,56},{56,64},{64,7... | collective-permute-start | bytes 786440 | tf_op jit(solution)/shard_map/while/body/eval_jaxpr/ppermute | solution.py:14
  662.7 9.8 %collective-permute-start = (f32[4,128,128]{2,1,0:T(8,128)S(1)}, f32[4,128,128]{2,1,0:T(8,128)S(1)}, u32[]{:S(2)}, u32[]{:S(2)}) collective-permute-start(f32[4,128,128]{2,1,0:T(8,128)S(1)} %get-tuple-element.260), channel_id=1, source_target_pairs={{0,8},{8,16},{16,24},{24,32},{32,40},{40,48},{48,56},{56,64},{64,7... | collective-permute-start | bytes 786440 | tf_op jit(solution)/shard_map/while/body/eval_jaxpr/ppermute | solution.py:14
  673.2 10.9 %collective-permute-start = (f32[4,128,128]{2,1,0:T(8,128)S(1)}, f32[4,128,128]{2,1,0:T(8,128)S(1)}, u32[]{:S(2)}, u32[]{:S(2)}) collective-permute-start(f32[4,128,128]{2,1,0:T(8,128)S(1)} %get-tuple-element.260), channel_id=1, source_target_pairs={{0,8},{8,16},{16,24},{24,32},{32,40},{40,48},{48,56},{56,64},{64,7... | collective-permute-start | bytes 786440 | tf_op jit(solution)/shard_map/while/body/eval_jaxpr/ppermute | solution.py:14
  684.7 12.2 %collective-permute-start = (f32[4,128,128]{2,1,0:T(8,128)S(1)}, f32[4,128,128]{2,1,0:T(8,128)S(1)}, u32[]{:S(2)}, u32[]{:S(2)}) collective-permute-start(f32[4,128,128]{2,1,0:T(8,128)S(1)} %get-tuple-element.260), channel_id=1, source_target_pairs={{0,8},{8,16},{16,24},{24,32},{32,40},{40,48},{48,56},{56,64},{64,7... | collective-permute-start | bytes 786440 | tf_op jit(solution)/shard_map/while/body/eval_jaxpr/ppermute | solution.py:14
  (100 other events, 423.8 us)
where the time goes:
time: 798 us; the launch traced here: 796 us
  waiting for transfers between devices  517 us (65%)
  starting transfers between devices  122 us (15%)
  blocking collectives  78.6 us (10%)
  local copies, waits for them, and re-layouts  50.7 us (6%)
  other arithmetic  21.6 us (3%)
    ppermute x63, waiting for transfers between devices, passed_along(): return lax.ppermute(block, axis, route)  517 us
    ppermute x63, starting transfers between devices, passed_along(): return lax.ppermute(block, axis, route)  122 us
    psum x1, blocking collectives, local(): lax.psum(jnp.sum(gated_out * gated_out, axis=1), 'head')  78.6 us
    while x126, local copies, waits for them, and re-layouts  38.2 us
  transfers between devices with their start and end apart: 63, of which 63 were waited for; matrix products, arithmetic and copies ran while one was open for 0% of the time, Pallas kernels for 0%

commit v1 on v0

v1 whole, which is shorter than its diff:
```python
import functools
import math

import jax
import jax.numpy as jnp
from jax import lax
from jax.experimental import pallas as pl
from jax.experimental.pallas import tpu as pltpu
from jax.sharding import Mesh
from jax.sharding import PartitionSpec as P

GROUP = 256
HALF = 128
LANES = 128
CODE_SCALE = 524288.0
CHANNELS = 4096
EPS = 1e-05
Y, Z, HEAD = 4, 16, 8
PIECE = 32
PIECE_ROWS = 40
MIB = 1 << 20
NT = (((1,), (1,)), ((), ()))
TN = (((0,), (0,)), ((), ()))


def matmul(a, b, dims=(((1,), (0,)), ((), ()))):
    return lax.dot_general(a, b, dims, preferred_element_type=jnp.float32)


def lower_triangle(size):
    row = lax.broadcasted_iota(jnp.int32, (size, size), 0)
    column = lax.broadcasted_iota(jnp.int32, (size, size), 1)
    return row >= column


def code_parts(codes, heads, blocks):
    rows = jnp.concatenate([codes[:, k * GROUP : (k + 1) * GROUP] for k in range(blocks)], axis=0)
    parts = [rows & 255, (rows >> 8) & 255, rows >> 16]
    return jnp.concatenate([part.astype(jnp.float32) for part in parts], axis=0).astype(jnp.bfloat16)


def joined(sums, axis):
    count = sums.shape[axis] // 3
    low, middle, high = (lax.slice_in_dim(sums, i * count, (i + 1) * count, axis=axis) for i in range(3))
    return low + 256.0 * middle + 65536.0 * high


def code_columns(parts, triangle):
    return joined(matmul(triangle, parts, NT), 1)


def code_rows(parts, triangle):
    return joined(matmul(parts, triangle, NT), 0)


def exponent_row(rate_ref, heads, blocks):
    lane = lax.broadcasted_iota(jnp.int32, (1, blocks * heads), 1)
    row = jnp.zeros((1, blocks * heads), jnp.float32)
    for h in range(heads):
        row = jnp.where(lax.rem(lane, heads) == h, rate_ref[h], row)
    return row * (-1.0 / (CODE_SCALE * math.log(2.0)))


def head_lanes(row, start, heads):
    return jnp.concatenate(
        [jnp.broadcast_to(row[:, start + h : start + h + 1], (1, LANES)) for h in range(heads)], axis=1
    )


def summary_kernel(heads, blocks, rate_ref, codes_ref, write_ref, x_ref, piece_ref, local_ref):
    triangle = lower_triangle(GROUP).astype(jnp.float32).astype(jnp.bfloat16)
    sums = code_columns(code_parts(codes_ref[...], heads, blocks), triangle)
    scale = exponent_row(rate_ref, heads, blocks)
    ends = sums[GROUP - 1 : GROUP, :]
    tail = jnp.exp2((ends - sums) * scale)
    block_decay = jnp.exp2(ends * scale)
    state = None
    for k in range(blocks):
        rows = pl.ds(k * GROUP, GROUP)
        weighted = jnp.concatenate(
            [
                (tail[:, k * heads + h : k * heads + h + 1] * x_ref[rows, h * LANES : (h + 1) * LANES].astype(jnp.float32))
                .astype(jnp.bfloat16)
                for h in range(heads)
            ],
            axis=1,
        )
        added = matmul(write_ref[rows, :], weighted, TN)
        if k:
            local_ref[k - 1] = state
            state = head_lanes(block_decay, k * heads, heads) * state + added
        else:
            state = added
    total = sum(ends[:, k * heads : (k + 1) * heads] for k in range(blocks))
    section_decay = jnp.exp2(total * scale[:, :heads])
    quarters = Z // heads
    for h in range(heads):
        decay = jnp.broadcast_to(section_decay[:, h : h + 1], (PIECE_ROWS - PIECE, LANES))
        for q in range(quarters):
            piece_ref[h * quarters + q, :PIECE, :] = state[q * PIECE : (q + 1) * PIECE, h * LANES : (h + 1) * LANES]
            piece_ref[h * quarters + q, PIECE:, :] = decay


def inner_kernel(
    heads, blocks, rate_ref, skip_ref, codes_ref, write_ref, read_ref, x_ref, gate_ref, base_ref, factor_ref, lead_ref
):
    causal = lower_triangle(GROUP)
    triangle = causal.astype(jnp.float32).astype(jnp.bfloat16)
    corner = lower_triangle(HALF)
    parts = code_parts(codes_ref[...], heads, blocks)
    columns = code_columns(parts, triangle)
    across = code_rows(parts, triangle)
    scale = exponent_row(rate_ref, heads, blocks)
    grown = jnp.exp2(columns * scale)
    ends = columns[GROUP - 1 : GROUP, :]
    before = jnp.zeros((1, heads), jnp.float32)
    for k in range(blocks):
        lead_ref[k : k + 1, :] = head_lanes(jnp.exp2(before * scale[:, :heads]), 0, heads)
        before = before + ends[:, k * heads : (k + 1) * heads]
    for k in range(blocks):
        rows = pl.ds(k * GROUP, GROUP)
        scores = matmul(read_ref[rows, :], write_ref[rows, :], NT)
        for h in range(heads):
            at = k * heads + h
            lanes = slice(h * LANES, (h + 1) * LANES)
            factor = scale[:, h : h + 1]
            column = columns[:, at : at + 1]
            row = across[at : at + 1, :]

            def mixed(t0, t1, s0, s1, masked):
                decay = jnp.exp2((column[t0:t1] - row[:, s0:s1]) * factor) * scores[t0:t1, s0:s1]
                if masked:
                    decay = jnp.where(corner, decay, 0.0)
                return decay.astype(jnp.bfloat16)

            x_part = x_ref[rows, lanes]
            upper = matmul(mixed(0, HALF, 0, HALF, True), x_part[:HALF])
            lower = jnp.concatenate(
                [mixed(HALF, GROUP, 0, HALF, False), mixed(HALF, GROUP, HALF, GROUP, True)], axis=1
            )
            inner = jnp.concatenate([upper, matmul(lower, x_part)], axis=0)
            gate = gate_ref[rows, lanes].astype(jnp.float32)
            silu = gate / (1.0 + jnp.exp(-gate))
            base_ref[rows, lanes] = (inner + skip_ref[h] * x_part.astype(jnp.float32)) * silu
            factor_ref[rows, lanes] = grown[:, at : at + 1] * silu


def scan_kernel(got_ref, prefix_ref, decay_ref, total_ref):
    state = jnp.zeros((PIECE, LANES), jnp.float32)
    decay = jnp.ones((PIECE_ROWS - PIECE, LANES), jnp.float32)
    for i in range(Z):
        prefix_ref[i] = state
        decay_ref[i] = decay
        step = got_ref[i, PIECE:, :]
        state = step[:1] * state + got_ref[i, :PIECE, :]
        decay = step * decay
    for j in range(Y):
        total_ref[j, :PIECE, :] = state
        total_ref[j, PIECE:, :] = decay


def join_kernel(totals_ref, prefix_ref, decay_ref, out_ref):
    mine = lax.axis_index("y")
    state = jnp.zeros((PIECE, LANES), jnp.float32)
    for j in range(Y - 1):
        state = jnp.where(j < mine, totals_ref[j, PIECE : PIECE + 1, :] * state + totals_ref[j, :PIECE, :], state)
    for i in range(Z):
        out_ref[i] = decay_ref[i, :1, :] * state + prefix_ref[i]


def carry_kernel(heads, blocks, entering_ref, local_ref, lead_ref, read_ref, base_ref, factor_ref, gated_ref, power_ref):
    quarters = Z // heads
    entering = jnp.concatenate(
        [
            jnp.concatenate([entering_ref[h * quarters + q] for q in range(quarters)], axis=0)
            for h in range(heads)
        ],
        axis=1,
    )
    sums = []
    for k in range(blocks):
        rows = pl.ds(k * GROUP, GROUP)
        state = lead_ref[k : k + 1, :] * entering + local_ref[k - 1] if k else entering
        read_out = matmul(read_ref[rows, :], state.astype(jnp.bfloat16))
        gated = base_ref[rows, :] + factor_ref[rows, :] * read_out
        gated_ref[rows, :] = gated
        squares = gated * gated
        squares = sum(squares[:, h * LANES : (h + 1) * LANES] for h in range(heads))
        for half in range(GROUP // LANES):
            sums.append(jnp.sum(squares[half * LANES : (half + 1) * LANES].T, axis=0, keepdims=True))
    sums = jnp.concatenate(sums, axis=0)
    for j in range(HEAD):
        power_ref[j] = sums


def norm_kernel(heads, power_ref, gain_ref, gated_ref, out_ref):
    power = sum(power_ref[j] for j in range(HEAD)) * (1.0 / CHANNELS)
    scale = lax.rsqrt(power + EPS)
    for r in range(scale.shape[0]):
        rows = pl.ds(r * LANES, LANES)
        column = jnp.broadcast_to(scale[r : r + 1, :], (LANES, LANES)).T
        for h in range(heads):
            lanes = slice(h * LANES, (h + 1) * LANES)
            out_ref[rows, lanes] = (gated_ref[rows, lanes] * column * gain_ref[:, lanes]).astype(jnp.bfloat16)


VMEM = pl.BlockSpec(memory_space=pltpu.VMEM)
SMEM = pl.BlockSpec(memory_space=pltpu.SMEM)


def call(kernel, out_shapes, in_specs, limit, flops, moved):
    return pl.pallas_call(
        kernel,
        out_shape=tuple(jax.ShapeDtypeStruct(shape, dtype) for shape, dtype in out_shapes),
        in_specs=in_specs,
        out_specs=tuple(VMEM for _ in out_shapes),
        compiler_params=pltpu.CompilerParams(vmem_limit_bytes=limit),
        cost_estimate=pl.CostEstimate(flops=flops, bytes_accessed=moved, transcendentals=0),
    )


def local(ssm_input, gate_input, write_proj, read_proj, decay_codes, decay_rate, skip_gain, norm_gain):
    rows, width = ssm_input.shape
    heads = decay_rate.shape[0]
    blocks = rows // GROUP
    f32 = jnp.float32
    piece, own = call(
        functools.partial(summary_kernel, heads, blocks),
        (((Z, PIECE_ROWS, LANES), f32), ((blocks - 1, LANES, width), f32)),
        [SMEM, VMEM, VMEM, VMEM],
        16 * MIB,
        1 << 28,
        3 * MIB,
    )(decay_rate, decay_codes, write_proj, ssm_input)
    got = lax.all_to_all(piece, "z", 0, 0, tiled=True)
    base, factor, lead = call(
        functools.partial(inner_kernel, heads, blocks),
        (((rows, width), f32), ((rows, width), f32), ((blocks, width), f32)),
        [SMEM, SMEM, VMEM, VMEM, VMEM, VMEM, VMEM],
        24 * MIB,
        1 << 30,
        7 * MIB,
    )(decay_rate, skip_gain, decay_codes, write_proj, read_proj, ssm_input, gate_input)
    prefix, prefix_decay, total = call(
        scan_kernel,
        (((Z, PIECE, LANES), f32), ((Z, PIECE_ROWS - PIECE, LANES), f32), ((Y, PIECE_ROWS, LANES), f32)),
        [VMEM],
        8 * MIB,
        1 << 20,
        MIB,
    )(got)
    totals = lax.all_to_all(total, "y", 0, 0, tiled=True)
    (joint,) = call(
        join_kernel, (((Z, PIECE, LANES), f32),), [VMEM, VMEM, VMEM], 8 * MIB, 1 << 20, MIB
    )(totals, prefix, prefix_decay)
    entering = lax.all_to_all(joint, "z", 0, 0, tiled=True)
    gated, power = call(
        functools.partial(carry_kernel, heads, blocks),
        (((rows, width), f32), ((HEAD, rows // LANES, LANES), f32)),
        [VMEM] * 6,
        16 * MIB,
        1 << 28,
        8 * MIB,
    )(entering, own, lead, read_proj, base, factor)
    powers = lax.all_to_all(power, "head", 0, 0, tiled=True)
    (out,) = call(
        functools.partial(norm_kernel, heads), (((rows, width), jnp.bfloat16),), [VMEM] * 3, 8 * MIB, 1 << 20, 3 * MIB
    )(powers, norm_gain.reshape(1, width), gated)
    return out


def solution(mesh):
    split = Mesh(mesh.devices.reshape(Y, Z, HEAD), ("y", "z", "head"))
    seq = ("y", "z")
    placed = (
        P(seq, "head"),
        P(seq, "head"),
        P(seq, None),
        P(seq, None),
        P("head", seq),
        P("head"),
        P("head"),
        P("head"),
    )
    return jax.shard_map(local, mesh=split, in_specs=placed, out_specs=P(seq, "head"), check_vma=False)
```

time: 798 us -> 91.7 us (0.11)
  the two profiles are of different devices: /device:TPU:25 before, /device:TPU:1 now
where the time goes in v1:
time: 91.7 us; the launch traced here: 91.1 us
  blocking collectives  55.1 us (60%)
  local copies, waits for them, and re-layouts  11.7 us (13%)
  starting transfers between devices  11.6 us (13%)
  Pallas kernels  6.9 us (8%)
  waiting for transfers between devices  5.71 us (6%)
    all_to_all x1, blocking collectives, local(): got = lax.all_to_all(piece, 'z', 0, 0, tiled=True)  30.8 us
    all_to_all x1, blocking collectives, local(): powers = lax.all_to_all(power, 'head', 0, 0, tiled=True)  15.8 us
    unnamed x34, local copies, waits for them, and re-layouts  11.7 us
    all_to_all x1, starting transfers between devices, local(): entering = lax.all_to_all(joint, 'z', 0, 0, tiled=True)  11.6 us
    all_to_all x1, blocking collectives, local(): totals = lax.all_to_all(total, 'y', 0, 0, tiled=True)  8.55 us
    all_to_all x1, waiting for transfers between devices, local(): entering = lax.all_to_all(joint, 'z', 0, 0, tiled=True)  5.71 us
    pallas_call x1, Pallas kernels, local(): call(functools.partial(inner_kernel, heads, blocks), (((rows, width), f32...  2.56 us
  transfers between devices with their start and end apart: 1, of which 1 were waited for; matrix products, arithmetic and copies ran while one was open for 0% of the time, Pallas kernels for 3%

profile of v1, /device:TPU:1, one launch (start us, length us, event | category | flops | bytes accessed | tf_op | source)
XLA Modules:
  0.0 91.1 jit_solution(15877930283328940695)
XLA Ops:
  0.0 0.0 copy-start.2
  0.0 1.2 %copy-done.2 = bf16[1024,512]{1,0:T(8,128)(2,1)S(1)} copy-done((bf16[1024,512]{1,0:T(8,128)(2,1)S(1)}, bf16[1024,512]{1,0:T(8,128)(2,1)}, u32[]{:S(2)}) %copy-start.2) | copy-done | bytes 1048600
  1.2 0.0 copy-start.6
  1.2 0.9 %copy-done.6 = bf16[1024,128]{1,0:T(8,128)(2,1)S(1)} copy-done((bf16[1024,128]{1,0:T(8,128)(2,1)S(1)}, bf16[1024,128]{1,0:T(8,128)(2,1)}, u32[]{:S(2)}) %copy-start.6) | copy-done | bytes 262168
  2.2 0.7 copy-done.10
  2.9 0.7 copy-done.13
  3.6 1.7 %shard_map.82 = (f32[16,40,128]{2,1,0:T(8,128)S(1)}, f32[3,128,512]{2,1,0:T(8,128)S(1)}) custom-call(f32[4]{0:T(128)S(1)} %copy-done.13, s32[4,1024]{1,0:T(4,128)S(1)} %copy-done.10, bf16[1024,128]{1,0:T(8,128)(2,1)S(1)} %copy-done.6, bf16[1024,512]{1,0:T(8,128)(2,1)S(1)} %copy-done.2), custom_call_target="tpu_custom_call" | custom-call | flops 268435456 | bytes 3145728 | tf_op jit(solution)/shard_map/pallas_call | solution.py:227
  5.3 0.0 copy-start.4
  5.3 30.8 %all_to_all.20.got_ref = f32[16,40,128]{2,1,0:T(8,128)S(1)} all-to-all(f32[16,40,128]{2,1,0:T(8,128)S(1)} %get-tuple-element.15), channel_id=1, replica_groups=mesh['y'=4,'z'=16,'head'=8] {'z'}, dimensions={0} | all-to-all | bytes 655360 | tf_op jit(solution)/shard_map/all_to_all | solution.py:235
  36.1 0.0 copy-done.4
  36.1 8.5 %all_to_all.21.totals_ref = f32[4,40,128]{2,1,0:T(8,128)S(1)} all-to-all(f32[4,40,128]{2,1,0:T(8,128)S(1)} %get-tuple-element.16), channel_id=1, replica_groups=mesh['y'=4,'z'=16,'head'=8] {'y'}, dimensions={0} | all-to-all | bytes 163840 | tf_op jit(solution)/shard_map/all_to_all | solution.py:252
  44.7 0.7 shard_map.84
  45.4 11.6 %all-to-all-start.2 = ((f32[16,32,128]{2,1,0:T(8,128)}), f32[16,32,128]{2,1,0:T(8,128)S(1)}, u32[]{:S(2)}, u32[]{:S(2)}) async-start(f32[16,32,128]{2,1,0:T(8,128)} %shard_map.84), calls=%async_computation.2 | async-start | bytes 524288 | tf_op jit(solution)/shard_map/all_to_all | solution.py:256
  57.0 0.0 copy-done.3
  57.0 0.0 copy-done.11
  57.0 0.0 copy-done.14
  57.0 0.0 copy-done.16
  57.0 0.0 copy-start.7
  57.1 0.9 %copy-done.7 = bf16[1024,128]{1,0:T(8,128)(2,1)S(1)} copy-done((bf16[1024,128]{1,0:T(8,128)(2,1)S(1)}, bf16[1024,128]{1,0:T(8,128)(2,1)}, u32[]{:S(2)}) %copy-start.7) | copy-done | bytes 262168
  58.0 0.9 %copy-done.8 = bf16[1024,128]{1,0:T(8,128)(2,1)S(1)} copy-done((bf16[1024,128]{1,0:T(8,128)(2,1)S(1)}, bf16[1024,128]{1,0:T(8,128)(2,1)}, u32[]{:S(2)}) %copy-start.8) | copy-done | bytes 262168
  59.0 1.2 %copy-done.15 = bf16[1024,512]{1,0:T(8,128)(2,1)S(1)} copy-done((bf16[1024,512]{1,0:T(8,128)(2,1)S(1)}, bf16[1024,512]{1,0:T(8,128)(2,1)}, u32[]{:S(2)}) %copy-start.15) | copy-done | bytes 1048600
  60.2 2.6 %shard_map.85 = (f32[1024,512]{1,0:T(8,128)S(1)}, f32[1024,512]{1,0:T(8,128)S(1)}, f32[4,512]{1,0:T(4,128)S(1)}) custom-call(f32[4]{0:T(128)S(1)} %copy-done.14, f32[4]{0:T(128)S(1)} %copy-done.16, s32[4,1024]{1,0:T(4,128)S(1)} %copy-done.11, bf16[1024,128]{1,0:T(8,128)(2,1)S(1)} %copy-done.7, bf16[1024,128]{1,0:T(8,128)(2,1)S(1)} %copy-done.8, ...), custom_call_target="tpu_custom_call" | custom-call | flops 1073741824 | bytes 7340032 | tf_op jit(solution)/shard_map/pallas_call | solution.py:236
  62.7 0.0 copy-start
  62.8 1.3 %copy-done = f32[1024,512]{1,0:T(8,128)} copy-done((f32[1024,512]{1,0:T(8,128)}, f32[1024,512]{1,0:T(8,128)S(1)}, u32[]{:S(2)}) %copy-start) | copy-done | bytes 2097176
  64.1 5.7 %all-to-all-done.2.entering_ref = f32[16,32,128]{2,1,0:T(8,128)S(1)} async-done(((f32[16,32,128]{2,1,0:T(8,128)}), f32[16,32,128]{2,1,0:T(8,128)S(1)}, u32[]{:S(2)}, u32[]{:S(2)}) %all-to-all-start.2) | async-done | bytes 262176 | tf_op jit(solution)/shard_map/all_to_all | solution.py:256
  69.8 1.6 %copy-done.1 = f32[1024,512]{1,0:T(8,128)S(1)} copy-done((f32[1024,512]{1,0:T(8,128)S(1)}, f32[1024,512]{1,0:T(8,128)}, u32[]{:S(2)}) %copy-start.1) | copy-done | bytes 2097176
  71.4 1.1 %copy-done.5 = f32[3,128,512]{2,1,0:T(8,128)S(1)} copy-done((f32[3,128,512]{2,1,0:T(8,128)S(1)}, f32[3,128,512]{2,1,0:T(8,128)}, u32[]{:S(2)}) %copy-start.5) | copy-done | bytes 786456
  72.5 0.9 %copy-done.9 = bf16[1024,128]{1,0:T(8,128)(2,1)S(1)} copy-done((bf16[1024,128]{1,0:T(8,128)(2,1)S(1)}, bf16[1024,128]{1,0:T(8,128)(2,1)}, u32[]{:S(2)}) %copy-start.9) | copy-done | bytes 262168
  73.5 0.5 shard_map.86
  74.0 15.8 %all_to_all.22.power_ref = f32[8,8,128]{2,1,0:T(8,128)S(1)} all-to-all(f32[8,8,128]{2,1,0:T(8,128)S(1)} %get-tuple-element.23), channel_id=1, replica_groups=mesh['y'=4,'z'=16,'head'=8] {'head'}, dimensions={0} | all-to-all | bytes 65536 | tf_op jit(solution)/shard_map/all_to_all | solution.py:265
  89.8 0.0 copy-done.12
  89.8 1.3 %shard_map.87 = bf16[1024,512]{1,0:T(8,128)(2,1)} custom-call(f32[8,8,128]{2,1,0:T(8,128)S(1)} %all_to_all.22.power_ref, f32[1,512]{1,0:T(1,128)S(1)} %bitcast.1, f32[1024,512]{1,0:T(8,128)S(1)} %get-tuple-element.24.gated_ref), custom_call_target="tpu_custom_call" | custom-call | flops 1048576 | bytes 3145728 | tf_op jit(solution)/shard_map/pallas_call | solution.py:266
  (13 shorter events, 0.1 us)
Async XLA Ops:
  0.0 1.2 %copy-start.2 = (bf16[1024,512]{1,0:T(8,128)(2,1)S(1)}, bf16[1024,512]{1,0:T(8,128)(2,1)}, u32[]{:S(2)}) copy-start(bf16[1024,512]{1,0:T(8,128)(2,1)} %x_ref.3) | copy-start | bytes 3145732
  1.2 0.9 %copy-start.6 = (bf16[1024,128]{1,0:T(8,128)(2,1)S(1)}, bf16[1024,128]{1,0:T(8,128)(2,1)}, u32[]{:S(2)}) copy-start(bf16[1024,128]{1,0:T(8,128)(2,1)} %write_ref.3) | copy-start | bytes 786436
  2.2 0.7 copy-start.10
  2.9 0.7 copy-start.13
  3.5 53.5 %copy-start.3 = (bf16[1024,512]{1,0:T(8,128)(2,1)S(1)}, bf16[1024,512]{1,0:T(8,128)(2,1)}, u32[]{:S(2)}) copy-start(bf16[1024,512]{1,0:T(8,128)(2,1)} %x_ref.3) | copy-start | bytes 3145732
  3.6 53.5 %copy-start.11 = (s32[4,1024]{1,0:T(4,128)S(1)}, s32[4,1024]{1,0:T(4,128)}, u32[]{:S(2)}) copy-start(s32[4,1024]{1,0:T(4,128)} %codes_ref.3) | copy-start | bytes 49156
  3.6 53.5 %copy-start.14 = (f32[4]{0:T(128)S(1)}, f32[4]{0:T(128)}, u32[]{:S(2)}) copy-start(f32[4]{0:T(128)} %rate_ref.3) | copy-start | bytes 52
  3.6 53.5 %copy-start.16 = (f32[4]{0:T(128)S(1)}, f32[4]{0:T(128)}, u32[]{:S(2)}) copy-start(f32[4]{0:T(128)} %skip_ref.1) | copy-start | bytes 52
  5.3 30.8 %copy-start.4 = (f32[3,128,512]{2,1,0:T(8,128)}, f32[3,128,512]{2,1,0:T(8,128)S(1)}, u32[]{:S(2)}) copy-start(f32[3,128,512]{2,1,0:T(8,128)S(1)} %get-tuple-element.19.local_ref) | copy-start | bytes 2359300
  45.4 24.4 %all-to-all-start.2 = ((f32[16,32,128]{2,1,0:T(8,128)}), f32[16,32,128]{2,1,0:T(8,128)S(1)}, u32[]{:S(2)}, u32[]{:S(2)}) async-start(f32[16,32,128]{2,1,0:T(8,128)} %shard_map.84), calls=%async_computation.2 | async-start | bytes 524288 | tf_op jit(solution)/shard_map/all_to_all | solution.py:256
  57.0 1.0 %copy-start.7 = (bf16[1024,128]{1,0:T(8,128)(2,1)S(1)}, bf16[1024,128]{1,0:T(8,128)(2,1)}, u32[]{:S(2)}) copy-start(bf16[1024,128]{1,0:T(8,128)(2,1)} %write_ref.3) | copy-start | bytes 786436
  58.0 0.9 %copy-start.8 = (bf16[1024,128]{1,0:T(8,128)(2,1)S(1)}, bf16[1024,128]{1,0:T(8,128)(2,1)}, u32[]{:S(2)}) copy-start(bf16[1024,128]{1,0:T(8,128)(2,1)} %read_ref.3) | copy-start | bytes 786436
  58.9 1.2 %copy-start.15 = (bf16[1024,512]{1,0:T(8,128)(2,1)S(1)}, bf16[1024,512]{1,0:T(8,128)(2,1)}, u32[]{:S(2)}) copy-start(bf16[1024,512]{1,0:T(8,128)(2,1)} %gate_ref.1) | copy-start | bytes 3145732
  62.7 1.3 %copy-start = (f32[1024,512]{1,0:T(8,128)}, f32[1024,512]{1,0:T(8,128)S(1)}, u32[]{:S(2)}) copy-start(f32[1024,512]{1,0:T(8,128)S(1)} %get-tuple-element.22.factor_ref) | copy-start | bytes 6291460
  69.8 1.6 %copy-start.1 = (f32[1024,512]{1,0:T(8,128)S(1)}, f32[1024,512]{1,0:T(8,128)}, u32[]{:S(2)}) copy-start(f32[1024,512]{1,0:T(8,128)} %copy-done) | copy-start | bytes 6291460
  71.4 1.1 %copy-start.5 = (f32[3,128,512]{2,1,0:T(8,128)S(1)}, f32[3,128,512]{2,1,0:T(8,128)}, u32[]{:S(2)}) copy-start(f32[3,128,512]{2,1,0:T(8,128)} %copy-done.4) | copy-start | bytes 2359300
  72.5 0.9 %copy-start.9 = (bf16[1024,128]{1,0:T(8,128)(2,1)S(1)}, bf16[1024,128]{1,0:T(8,128)(2,1)}, u32[]{:S(2)}) copy-start(bf16[1024,128]{1,0:T(8,128)(2,1)} %read_ref.3) | copy-start | bytes 786436
  73.5 16.3 %copy-start.12 = (f32[512]{0:T(512)S(1)}, f32[512]{0:T(512)}, u32[]{:S(2)}) copy-start(f32[512]{0:T(512)} %param.15) | copy-start | bytes 6148

commit v2 on v1

--- a/solution.py
+++ b/solution.py
@@ -67,16 +67,49 @@
     )
 
 
-def summary_kernel(heads, blocks, rate_ref, codes_ref, write_ref, x_ref, piece_ref, local_ref):
+def summary_kernel(
+    heads,
+    blocks,
+    rate_hbm,
+    codes_hbm,
+    write_hbm,
+    x_hbm,
+    piece_ref,
+    local_ref,
+    rate_ref,
+    codes_ref,
+    write_ref,
+    x_ref,
+    small_sem,
+    write_sem,
+    x_sem,
+):
+    small = [
+        pltpu.make_async_copy(rate_hbm, rate_ref, small_sem.at[0]),
+        pltpu.make_async_copy(codes_hbm, codes_ref, small_sem.at[1]),
+    ]
+    parts_of = [pl.ds(k * GROUP, GROUP) for k in range(blocks)]
+    writes = [
+        pltpu.make_async_copy(write_hbm.at[rows], write_ref.at[rows], write_sem.at[k]) for k, rows in enumerate(parts_of)
+    ]
+    inputs = [pltpu.make_async_copy(x_hbm.at[rows], x_ref.at[rows], x_sem.at[k]) for k, rows in enumerate(parts_of)]
+    for copy in small:
+        copy.start()
+    for k in range(blocks):
+        writes[k].start()
+        inputs[k].start()
     triangle = lower_triangle(GROUP).astype(jnp.float32).astype(jnp.bfloat16)
+    for copy in small:
+        copy.wait()
     sums = code_columns(code_parts(codes_ref[...], heads, blocks), triangle)
     scale = exponent_row(rate_ref, heads, blocks)
     ends = sums[GROUP - 1 : GROUP, :]
     tail = jnp.exp2((ends - sums) * scale)
     block_decay = jnp.exp2(ends * scale)
     state = None
-    for k in range(blocks):
-        rows = pl.ds(k * GROUP, GROUP)
+    for k, rows in enumerate(parts_of):
+        writes[k].wait()
+        inputs[k].wait()
         weighted = jnp.concatenate(
             [
                 (tail[:, k * heads + h : k * heads + h + 1] * x_ref[rows, h * LANES : (h + 1) * LANES].astype(jnp.float32))
@@ -193,27 +226,34 @@
         power_ref[j] = sums
 
 
-def norm_kernel(heads, power_ref, gain_ref, gated_ref, out_ref):
+def norm_kernel(heads, power_ref, gain_ref, gated_ref, out_hbm, out_ref, out_sem):
     power = sum(power_ref[j] for j in range(HEAD)) * (1.0 / CHANNELS)
     scale = lax.rsqrt(power + EPS)
+    copies = []
     for r in range(scale.shape[0]):
         rows = pl.ds(r * LANES, LANES)
         column = jnp.broadcast_to(scale[r : r + 1, :], (LANES, LANES)).T
         for h in range(heads):
             lanes = slice(h * LANES, (h + 1) * LANES)
             out_ref[rows, lanes] = (gated_ref[rows, lanes] * column * gain_ref[:, lanes]).astype(jnp.bfloat16)
+        copies.append(pltpu.make_async_copy(out_ref.at[rows], out_hbm.at[rows], out_sem.at[r]))
+        copies[-1].start()
+    for copy in copies:
+        copy.wait()
 
 
 VMEM = pl.BlockSpec(memory_space=pltpu.VMEM)
 SMEM = pl.BlockSpec(memory_space=pltpu.SMEM)
-
-
-def call(kernel, out_shapes, in_specs, limit, flops, moved):
+HBM = pl.BlockSpec(memory_space=pltpu.HBM)
+
+
+def call(kernel, out_shapes, in_specs, limit, flops, moved, scratch=(), out_spec=VMEM):
     return pl.pallas_call(
         kernel,
         out_shape=tuple(jax.ShapeDtypeStruct(shape, dtype) for shape, dtype in out_shapes),
         in_specs=in_specs,
-        out_specs=tuple(VMEM for _ in out_shapes),
+        out_specs=tuple(out_spec for _ in out_shapes),
+        scratch_shapes=scratch,
         compiler_params=pltpu.CompilerParams(vmem_limit_bytes=limit),
         cost_estimate=pl.CostEstimate(flops=flops, bytes_accessed=moved, transcendentals=0),
     )
@@ -227,11 +267,20 @@
     piece, own = call(
         functools.partial(summary_kernel, heads, blocks),
         (((Z, PIECE_ROWS, LANES), f32), ((blocks - 1, LANES, width), f32)),
-        [SMEM, VMEM, VMEM, VMEM],
-        16 * MIB,
+        [HBM] * 4,
+        8 * MIB,
         1 << 28,
         3 * MIB,
-    )(decay_rate, decay_codes, write_proj, ssm_input)
+        (
+            pltpu.SMEM(decay_rate.shape, f32),
+            pltpu.VMEM(decay_codes.shape, jnp.int32),
+            pltpu.VMEM(write_proj.shape, jnp.bfloat16),
+            pltpu.VMEM(ssm_input.shape, jnp.bfloat16),
+            pltpu.SemaphoreType.DMA((2,)),
+            pltpu.SemaphoreType.DMA((blocks,)),
+            pltpu.SemaphoreType.DMA((blocks,)),
+        ),
+    )(*(pltpu.with_memory_space_constraint(a, pltpu.HBM) for a in (decay_rate, decay_codes, write_proj, ssm_input)))
     got = lax.all_to_all(piece, "z", 0, 0, tiled=True)
     base, factor, lead = call(
         functools.partial(inner_kernel, heads, blocks),
@@ -241,17 +290,18 @@
         1 << 30,
         7 * MIB,
     )(decay_rate, skip_gain, decay_codes, write_proj, read_proj, ssm_input, gate_input)
+    got, base, factor, lead = lax.optimization_barrier((got, base, factor, lead))
     prefix, prefix_decay, total = call(
         scan_kernel,
         (((Z, PIECE, LANES), f32), ((Z, PIECE_ROWS - PIECE, LANES), f32), ((Y, PIECE_ROWS, LANES), f32)),
         [VMEM],
         8 * MIB,
-        1 << 20,
+        1 << 33,
         MIB,
     )(got)
     totals = lax.all_to_all(total, "y", 0, 0, tiled=True)
     (joint,) = call(
-        join_kernel, (((Z, PIECE, LANES), f32),), [VMEM, VMEM, VMEM], 8 * MIB, 1 << 20, MIB
+        join_kernel, (((Z, PIECE, LANES), f32),), [VMEM, VMEM, VMEM], 8 * MIB, 1 << 33, MIB
     )(totals, prefix, prefix_decay)
     entering = lax.all_to_all(joint, "z", 0, 0, tiled=True)
     gated, power = call(
@@ -264,7 +314,14 @@
     )(entering, own, lead, read_proj, base, factor)
     powers = lax.all_to_all(power, "head", 0, 0, tiled=True)
     (out,) = call(
-        functools.partial(norm_kernel, heads), (((rows, width), jnp.bfloat16),), [VMEM] * 3, 8 * MIB, 1 << 20, 3 * MIB
+        functools.partial(norm_kernel, heads),
+        (((rows, width), jnp.bfloat16),),
+        [VMEM] * 3,
+        8 * MIB,
+        1 << 20,
+        3 * MIB,
+        (pltpu.VMEM((rows, width), jnp.bfloat16), pltpu.SemaphoreType.DMA((rows // LANES,))),
+        HBM,
     )(powers, norm_gain.reshape(1, width), gated)
     return out
 

time: 91.7 us -> 85.8 us (0.936)
  blocking collectives: 55.1 us -> 48.6 us
  starting transfers between devices: 11.6 us -> 15.8 us
  local copies, waits for them, and re-layouts: 11.7 us -> 7.71 us
  Pallas kernels: 6.9 us -> 8.29 us
    all_to_all x1, blocking collectives: 30.8 us -> 24.3 us  [local(): entering = lax.all_to_all(joint, 'z', 0, 0, tiled=True)]
    all_to_all x1, starting transfers between devices: 11.6 us -> 15.8 us  [local(): got = lax.all_to_all(piece, 'z', 0, 0, tiled=True)]
    unnamed x34 -> x22, local copies, waits for them, and re-layouts: 11.7 us -> 7.71 us
    pallas_call x1, Pallas kernels: 1.72 us -> 3.88 us  [local(): call(functools.partial(summary_kernel, heads, blocks), (((Z, PIECE_ROWS,...]
where the time goes in v2:
time: 85.8 us; the launch traced here: 85.3 us
  blocking collectives  48.6 us (57%)
  starting transfers between devices  15.8 us (18%)
  Pallas kernels  8.29 us (10%)
  local copies, waits for them, and re-layouts  7.71 us (9%)
  waiting for transfers between devices  4.89 us (6%)
    all_to_all x1, blocking collectives, local(): entering = lax.all_to_all(joint, 'z', 0, 0, tiled=True)  24.3 us
    all_to_all x1, blocking collectives, local(): powers = lax.all_to_all(power, 'head', 0, 0, tiled=True)  15.8 us
    all_to_all x1, starting transfers between devices, local(): got = lax.all_to_all(piece, 'z', 0, 0, tiled=True)  15.8 us
    all_to_all x1, blocking collectives, local(): totals = lax.all_to_all(total, 'y', 0, 0, tiled=True)  8.55 us
    unnamed x22, local copies, waits for them, and re-layouts  7.71 us
    all_to_all x1, waiting for transfers between devices, local(): got = lax.all_to_all(piece, 'z', 0, 0, tiled=True)  4.89 us
    pallas_call x1, Pallas kernels, local(): call(functools.partial(summary_kernel, heads, blocks), (((Z, PIECE_ROWS,...  3.88 us
    pallas_call x1, Pallas kernels, local(): call(functools.partial(inner_kernel, heads, blocks), (((rows, width), f32...  2.62 us
  transfers between devices with their start and end apart: 1, of which 1 were waited for; matrix products, arithmetic and copies ran while one was open for 0% of the time, Pallas kernels for 3%

profile of v2, /device:TPU:1, one launch (start us, length us, event | category | flops | bytes accessed | tf_op | source)
XLA Modules:
  0.0 85.3 jit_solution(17592647649041451991)
XLA Ops:
  0.0 3.9 %shard_map.82 = (f32[16,40,128]{2,1,0:T(8,128)}, f32[3,128,512]{2,1,0:T(8,128)S(1)}) custom-call(f32[4]{0:T(128)} %rate_ref.1, s32[4,1024]{1,0:T(4,128)} %codes_ref.1, bf16[1024,128]{1,0:T(8,128)(2,1)} %write_ref.1, bf16[1024,512]{1,0:T(8,128)(2,1)} %x_ref.1), custom_call_target="tpu_custom_call" | custom-call | flops 268435456 | bytes 3145728 | tf_op jit(solution)/shard_map/pallas_call | solution.py:267
  3.9 15.8 %all-to-all-start = ((f32[16,40,128]{2,1,0:T(8,128)}), f32[16,40,128]{2,1,0:T(8,128)S(1)}, u32[]{:S(2)}, u32[]{:S(2)}) async-start(f32[16,40,128]{2,1,0:T(8,128)} %get-tuple-element.19), calls=%async_computation | async-start | bytes 655360 | tf_op jit(solution)/shard_map/all_to_all | solution.py:284
  19.6 0.0 copy-start.2
  19.7 1.2 %copy-done.2 = bf16[1024,512]{1,0:T(8,128)(2,1)S(1)} copy-done((bf16[1024,512]{1,0:T(8,128)(2,1)S(1)}, bf16[1024,512]{1,0:T(8,128)(2,1)}, u32[]{:S(2)}) %copy-start.2) | copy-done | bytes 1048600
  20.9 0.0 copy-start.3
  20.9 0.9 %copy-done.3 = bf16[1024,128]{1,0:T(8,128)(2,1)S(1)} copy-done((bf16[1024,128]{1,0:T(8,128)(2,1)S(1)}, bf16[1024,128]{1,0:T(8,128)(2,1)}, u32[]{:S(2)}) %copy-start.3) | copy-done | bytes 262168
  21.8 0.0 copy-start.4
  21.8 0.9 %copy-done.4 = bf16[1024,128]{1,0:T(8,128)(2,1)S(1)} copy-done((bf16[1024,128]{1,0:T(8,128)(2,1)S(1)}, bf16[1024,128]{1,0:T(8,128)(2,1)}, u32[]{:S(2)}) %copy-start.4) | copy-done | bytes 262168
  22.8 0.0 copy-start.6
  22.8 0.7 copy-done.6
  23.5 0.0 copy-start.8
  23.5 0.7 copy-done.8
  24.2 0.0 copy-start.9
  24.2 1.2 %copy-done.9 = bf16[1024,512]{1,0:T(8,128)(2,1)S(1)} copy-done((bf16[1024,512]{1,0:T(8,128)(2,1)S(1)}, bf16[1024,512]{1,0:T(8,128)(2,1)}, u32[]{:S(2)}) %copy-start.9) | copy-done | bytes 1048600
  25.4 0.0 copy-start.10
  25.4 0.7 copy-done.10
  26.0 2.6 %shard_map.83 = (f32[1024,512]{1,0:T(8,128)S(1)}, f32[1024,512]{1,0:T(8,128)S(1)}, f32[4,512]{1,0:T(4,128)S(1)}) custom-call(f32[4]{0:T(128)S(1)} %copy-done.8, f32[4]{0:T(128)S(1)} %copy-done.10, s32[4,1024]{1,0:T(4,128)S(1)} %copy-done.6, bf16[1024,128]{1,0:T(8,128)(2,1)S(1)} %copy-done.3, bf16[1024,128]{1,0:T(8,128)(2,1)S(1)} %copy-done.4, ...), custom_call_target="tpu_custom_call" | custom-call | flops 1073741824 | bytes 7340032 | tf_op jit(solution)/shard_map/pallas_call | solution.py:285
  28.7 0.0 copy-start
  28.7 1.3 %copy-done = f32[1024,512]{1,0:T(8,128)} copy-done((f32[1024,512]{1,0:T(8,128)}, f32[1024,512]{1,0:T(8,128)S(1)}, u32[]{:S(2)}) %copy-start) | copy-done | bytes 2097176
  30.0 4.9 %all-to-all-done.got_ref = f32[16,40,128]{2,1,0:T(8,128)S(1)} async-done(((f32[16,40,128]{2,1,0:T(8,128)}), f32[16,40,128]{2,1,0:T(8,128)S(1)}, u32[]{:S(2)}, u32[]{:S(2)}) %all-to-all-start) | async-done | bytes 327712 | tf_op jit(solution)/shard_map/all_to_all | solution.py:284
  34.9 8.6 %all_to_all.20.totals_ref = f32[4,40,128]{2,1,0:T(8,128)S(1)} all-to-all(f32[4,40,128]{2,1,0:T(8,128)S(1)} %get-tuple-element.24), channel_id=1, replica_groups=mesh['y'=4,'z'=16,'head'=8] {'y'}, dimensions={0} | all-to-all | bytes 163840 | tf_op jit(solution)/shard_map/all_to_all | solution.py:302
  43.5 0.0 copy-start.1
  43.5 0.0 copy-start.5
  43.5 24.3 %all_to_all.21.entering_ref = f32[16,32,128]{2,1,0:T(8,128)S(1)} all-to-all(f32[16,32,128]{2,1,0:T(8,128)S(1)} %shard_map.85), channel_id=1, replica_groups=mesh['y'=4,'z'=16,'head'=8] {'z'}, dimensions={0} | all-to-all | bytes 524288 | tf_op jit(solution)/shard_map/all_to_all | solution.py:306
  67.8 0.0 copy-done.1
  67.8 0.0 copy-done.5
  67.8 0.0 copy-start.7
  67.8 0.6 shard_map.86
  68.4 15.8 %all_to_all.22.power_ref = f32[8,8,128]{2,1,0:T(8,128)S(1)} all-to-all(f32[8,8,128]{2,1,0:T(8,128)S(1)} %get-tuple-element.31), channel_id=1, replica_groups=mesh['y'=4,'z'=16,'head'=8] {'head'}, dimensions={0} | all-to-all | bytes 65536 | tf_op jit(solution)/shard_map/all_to_all | solution.py:315
  84.1 0.0 copy-done.7
  84.1 1.2 %shard_map.87 = bf16[1024,512]{1,0:T(8,128)(2,1)} custom-call(f32[8,8,128]{2,1,0:T(8,128)S(1)} %all_to_all.22.power_ref, f32[1,512]{1,0:T(1,128)S(1)} %bitcast.1, f32[1024,512]{1,0:T(8,128)S(1)} %get-tuple-element.32.gated_ref), custom_call_target="tpu_custom_call" | custom-call | flops 1048576 | bytes 3145728 | tf_op jit(solution)/shard_map/pallas_call | solution.py:316
  (2 shorter events, 0.1 us)
Async XLA Ops:
  3.9 31.0 %all-to-all-start = ((f32[16,40,128]{2,1,0:T(8,128)}), f32[16,40,128]{2,1,0:T(8,128)S(1)}, u32[]{:S(2)}, u32[]{:S(2)}) async-start(f32[16,40,128]{2,1,0:T(8,128)} %get-tuple-element.19), calls=%async_computation | async-start | bytes 655360 | tf_op jit(solution)/shard_map/all_to_all | solution.py:284
  19.6 1.2 %copy-start.2 = (bf16[1024,512]{1,0:T(8,128)(2,1)S(1)}, bf16[1024,512]{1,0:T(8,128)(2,1)}, u32[]{:S(2)}) copy-start(bf16[1024,512]{1,0:T(8,128)(2,1)} %x_ref.1) | copy-start | bytes 3145732
  20.9 0.9 %copy-start.3 = (bf16[1024,128]{1,0:T(8,128)(2,1)S(1)}, bf16[1024,128]{1,0:T(8,128)(2,1)}, u32[]{:S(2)}) copy-start(bf16[1024,128]{1,0:T(8,128)(2,1)} %write_ref.1) | copy-start | bytes 786436
  21.8 0.9 %copy-start.4 = (bf16[1024,128]{1,0:T(8,128)(2,1)S(1)}, bf16[1024,128]{1,0:T(8,128)(2,1)}, u32[]{:S(2)}) copy-start(bf16[1024,128]{1,0:T(8,128)(2,1)} %read_ref.3) | copy-start | bytes 786436
  22.8 0.7 copy-start.6
  23.5 0.7 copy-start.8
  24.2 1.2 %copy-start.9 = (bf16[1024,512]{1,0:T(8,128)(2,1)S(1)}, bf16[1024,512]{1,0:T(8,128)(2,1)}, u32[]{:S(2)}) copy-start(bf16[1024,512]{1,0:T(8,128)(2,1)} %gate_ref.1) | copy-start | bytes 3145732
  25.4 0.7 copy-start.10
  28.7 1.3 %copy-start = (f32[1024,512]{1,0:T(8,128)}, f32[1024,512]{1,0:T(8,128)S(1)}, u32[]{:S(2)}) copy-start(f32[1024,512]{1,0:T(8,128)S(1)} %get-tuple-element.30.factor_ref) | copy-start | bytes 6291460
  43.5 24.3 %copy-start.1 = (f32[1024,512]{1,0:T(8,128)S(1)}, f32[1024,512]{1,0:T(8,128)}, u32[]{:S(2)}) copy-start(f32[1024,512]{1,0:T(8,128)} %copy-done) | copy-start | bytes 6291460
  43.5 24.3 %copy-start.5 = (bf16[1024,128]{1,0:T(8,128)(2,1)S(1)}, bf16[1024,128]{1,0:T(8,128)(2,1)}, u32[]{:S(2)}) copy-start(bf16[1024,128]{1,0:T(8,128)(2,1)} %read_ref.3) | copy-start | bytes 786436
  67.8 16.3 %copy-start.7 = (f32[512]{0:T(512)S(1)}, f32[512]{0:T(512)}, u32[]{:S(2)}) copy-start(f32[512]{0:T(512)} %param.15) | copy-start | bytes 6148

commit v3 on v2

--- a/solution.py
+++ b/solution.py
@@ -15,9 +15,9 @@
 CODE_SCALE = 524288.0
 CHANNELS = 4096
 EPS = 1e-05
-Y, Z, HEAD = 4, 16, 8
-PIECE = 32
-PIECE_ROWS = 40
+Y, FAR, NEAR, HEAD = 4, 4, 4, 8
+STATE = 128
+PIECE_ROWS = 136
 MIB = 1 << 20
 NT = (((1,), (1,)), ((), ()))
 TN = (((0,), (0,)), ((), ()))
@@ -126,17 +126,40 @@
             state = added
     total = sum(ends[:, k * heads : (k + 1) * heads] for k in range(blocks))
     section_decay = jnp.exp2(total * scale[:, :heads])
-    quarters = Z // heads
     for h in range(heads):
-        decay = jnp.broadcast_to(section_decay[:, h : h + 1], (PIECE_ROWS - PIECE, LANES))
-        for q in range(quarters):
-            piece_ref[h * quarters + q, :PIECE, :] = state[q * PIECE : (q + 1) * PIECE, h * LANES : (h + 1) * LANES]
-            piece_ref[h * quarters + q, PIECE:, :] = decay
+        piece_ref[h, :STATE, :] = state[:, h * LANES : (h + 1) * LANES]
+        piece_ref[h, STATE:, :] = jnp.broadcast_to(section_decay[:, h : h + 1], (PIECE_ROWS - STATE, LANES))
 
 
 def inner_kernel(
-    heads, blocks, rate_ref, skip_ref, codes_ref, write_ref, read_ref, x_ref, gate_ref, base_ref, factor_ref, lead_ref
+    heads,
+    blocks,
+    rate_hbm,
+    skip_hbm,
+    codes_hbm,
+    write_hbm,
+    read_hbm,
+    x_hbm,
+    gate_hbm,
+    base_ref,
+    factor_ref,
+    lead_ref,
+    rate_ref,
+    skip_ref,
+    codes_ref,
+    write_ref,
+    read_ref,
+    x_ref,
+    gate_ref,
+    sem,
 ):
+    sources = (rate_hbm, skip_hbm, codes_hbm, write_hbm, read_hbm, x_hbm, gate_hbm)
+    targets = (rate_ref, skip_ref, codes_ref, write_ref, read_ref, x_ref, gate_ref)
+    copies = [pltpu.make_async_copy(a, b, sem.at[i]) for i, (a, b) in enumerate(zip(sources, targets, strict=True))]
+    for copy in copies:
+        copy.start()
+    for copy in copies:
+        copy.wait()
     causal = lower_triangle(GROUP)
     triangle = causal.astype(jnp.float32).astype(jnp.bfloat16)
     corner = lower_triangle(HALF)
@@ -178,38 +201,50 @@
             factor_ref[rows, lanes] = grown[:, at : at + 1] * silu
 
 
-def scan_kernel(got_ref, prefix_ref, decay_ref, total_ref):
-    state = jnp.zeros((PIECE, LANES), jnp.float32)
-    decay = jnp.ones((PIECE_ROWS - PIECE, LANES), jnp.float32)
-    for i in range(Z):
+def near_kernel(got_ref, prefix_ref, decay_ref, total_ref):
+    state = jnp.zeros((STATE, LANES), jnp.float32)
+    decay = jnp.ones((PIECE_ROWS - STATE, LANES), jnp.float32)
+    for i in range(NEAR):
         prefix_ref[i] = state
         decay_ref[i] = decay
-        step = got_ref[i, PIECE:, :]
-        state = step[:1] * state + got_ref[i, :PIECE, :]
+        step = got_ref[i, STATE:, :]
+        state = step[:1] * state + got_ref[i, :STATE, :]
         decay = step * decay
+    for j in range(FAR):
+        total_ref[j, :STATE, :] = state
+        total_ref[j, STATE:, :] = decay
+
+
+def far_kernel(got_ref, prefix_ref, total_ref):
+    mine = lax.axis_index("far")
+    state = jnp.zeros((STATE, LANES), jnp.float32)
+    decay = jnp.ones((PIECE_ROWS - STATE, LANES), jnp.float32)
+    own, own_decay = state, decay
+    for i in range(FAR):
+        own = jnp.where(i == mine, state, own)
+        own_decay = jnp.where(i == mine, decay, own_decay)
+        step = got_ref[i, STATE:, :]
+        state = step[:1] * state + got_ref[i, :STATE, :]
+        decay = step * decay
+    prefix_ref[:STATE, :] = own
+    prefix_ref[STATE:, :] = own_decay
     for j in range(Y):
-        total_ref[j, :PIECE, :] = state
-        total_ref[j, PIECE:, :] = decay
-
-
-def join_kernel(totals_ref, prefix_ref, decay_ref, out_ref):
+        total_ref[j, :STATE, :] = state
+        total_ref[j, STATE:, :] = decay
+
+
+def join_kernel(totals_ref, group_ref, prefix_ref, decay_ref, out_ref):
     mine = lax.axis_index("y")
-    state = jnp.zeros((PIECE, LANES), jnp.float32)
+    state = jnp.zeros((STATE, LANES), jnp.float32)
     for j in range(Y - 1):
-        state = jnp.where(j < mine, totals_ref[j, PIECE : PIECE + 1, :] * state + totals_ref[j, :PIECE, :], state)
-    for i in range(Z):
+        state = jnp.where(j < mine, totals_ref[j, STATE : STATE + 1, :] * state + totals_ref[j, :STATE, :], state)
+    state = group_ref[STATE : STATE + 1, :] * state + group_ref[:STATE, :]
+    for i in range(NEAR):
         out_ref[i] = decay_ref[i, :1, :] * state + prefix_ref[i]
 
 
 def carry_kernel(heads, blocks, entering_ref, local_ref, lead_ref, read_ref, base_ref, factor_ref, gated_ref, power_ref):
-    quarters = Z // heads
-    entering = jnp.concatenate(
-        [
-            jnp.concatenate([entering_ref[h * quarters + q] for q in range(quarters)], axis=0)
-            for h in range(heads)
-        ],
-        axis=1,
-    )
+    entering = jnp.concatenate([entering_ref[h] for h in range(heads)], axis=1)
     sums = []
     for k in range(blocks):
         rows = pl.ds(k * GROUP, GROUP)
@@ -259,14 +294,18 @@
     )
 
 
+def in_hbm(*arrays):
+    return tuple(pltpu.with_memory_space_constraint(array, pltpu.HBM) for array in arrays)
+
+
 def local(ssm_input, gate_input, write_proj, read_proj, decay_codes, decay_rate, skip_gain, norm_gain):
     rows, width = ssm_input.shape
     heads = decay_rate.shape[0]
     blocks = rows // GROUP
-    f32 = jnp.float32
+    f32, bf16 = jnp.float32, jnp.bfloat16
     piece, own = call(
         functools.partial(summary_kernel, heads, blocks),
-        (((Z, PIECE_ROWS, LANES), f32), ((blocks - 1, LANES, width), f32)),
+        (((NEAR, PIECE_ROWS, LANES), f32), ((blocks - 1, LANES, width), f32)),
         [HBM] * 4,
         8 * MIB,
         1 << 28,
@@ -274,36 +313,56 @@
         (
             pltpu.SMEM(decay_rate.shape, f32),
             pltpu.VMEM(decay_codes.shape, jnp.int32),
-            pltpu.VMEM(write_proj.shape, jnp.bfloat16),
-            pltpu.VMEM(ssm_input.shape, jnp.bfloat16),
+            pltpu.VMEM(write_proj.shape, bf16),
+            pltpu.VMEM(ssm_input.shape, bf16),
             pltpu.SemaphoreType.DMA((2,)),
             pltpu.SemaphoreType.DMA((blocks,)),
             pltpu.SemaphoreType.DMA((blocks,)),
         ),
-    )(*(pltpu.with_memory_space_constraint(a, pltpu.HBM) for a in (decay_rate, decay_codes, write_proj, ssm_input)))
-    got = lax.all_to_all(piece, "z", 0, 0, tiled=True)
+    )(*in_hbm(decay_rate, decay_codes, write_proj, ssm_input))
+    got = lax.all_to_all(piece, "near", 0, 0, tiled=True)
+    got, later_gate = lax.optimization_barrier((got, gate_input))
+    prefix, prefix_decay, total = call(
+        near_kernel,
+        (((NEAR, STATE, LANES), f32), ((NEAR, PIECE_ROWS - STATE, LANES), f32), ((FAR, PIECE_ROWS, LANES), f32)),
+        [VMEM],
+        8 * MIB,
+        1 << 20,
+        MIB,
+    )(got)
+    totals = lax.all_to_all(total, "far", 0, 0, tiled=True)
     base, factor, lead = call(
         functools.partial(inner_kernel, heads, blocks),
         (((rows, width), f32), ((rows, width), f32), ((blocks, width), f32)),
-        [SMEM, SMEM, VMEM, VMEM, VMEM, VMEM, VMEM],
-        24 * MIB,
+        [HBM] * 7,
+        16 * MIB,
         1 << 30,
         7 * MIB,
-    )(decay_rate, skip_gain, decay_codes, write_proj, read_proj, ssm_input, gate_input)
-    got, base, factor, lead = lax.optimization_barrier((got, base, factor, lead))
-    prefix, prefix_decay, total = call(
-        scan_kernel,
-        (((Z, PIECE, LANES), f32), ((Z, PIECE_ROWS - PIECE, LANES), f32), ((Y, PIECE_ROWS, LANES), f32)),
+        (
+            pltpu.SMEM(decay_rate.shape, f32),
+            pltpu.SMEM(skip_gain.shape, f32),
+            pltpu.VMEM(decay_codes.shape, jnp.int32),
+            pltpu.VMEM(write_proj.shape, bf16),
+            pltpu.VMEM(read_proj.shape, bf16),
+            pltpu.VMEM(ssm_input.shape, bf16),
+            pltpu.VMEM(gate_input.shape, bf16),
+            pltpu.SemaphoreType.DMA((7,)),
+        ),
+    )(*in_hbm(decay_rate, skip_gain, decay_codes, write_proj, read_proj, ssm_input, later_gate))
+    totals, base, factor, lead = lax.optimization_barrier((totals, base, factor, lead))
+    group, row_total = call(
+        far_kernel,
+        (((PIECE_ROWS, LANES), f32), ((Y, PIECE_ROWS, LANES), f32)),
         [VMEM],
         8 * MIB,
         1 << 33,
         MIB,
-    )(got)
-    totals = lax.all_to_all(total, "y", 0, 0, tiled=True)
-    (joint,) = call(
-        join_kernel, (((Z, PIECE, LANES), f32),), [VMEM, VMEM, VMEM], 8 * MIB, 1 << 33, MIB
-    )(totals, prefix, prefix_decay)
-    entering = lax.all_to_all(joint, "z", 0, 0, tiled=True)
+    )(totals)
+    row_totals = lax.all_to_all(row_total, "y", 0, 0, tiled=True)
+    (joint,) = call(join_kernel, (((NEAR, STATE, LANES), f32),), [VMEM] * 4, 8 * MIB, 1 << 33, MIB)(
+        row_totals, group, prefix, prefix_decay
+    )
+    entering = lax.all_to_all(joint, "near", 0, 0, tiled=True)
     gated, power = call(
         functools.partial(carry_kernel, heads, blocks),
         (((rows, width), f32), ((HEAD, rows // LANES, LANES), f32)),
@@ -315,20 +374,20 @@
     powers = lax.all_to_all(power, "head", 0, 0, tiled=True)
     (out,) = call(
         functools.partial(norm_kernel, heads),
-        (((rows, width), jnp.bfloat16),),
+        (((rows, width), bf16),),
         [VMEM] * 3,
         8 * MIB,
         1 << 20,
         3 * MIB,
-        (pltpu.VMEM((rows, width), jnp.bfloat16), pltpu.SemaphoreType.DMA((rows // LANES,))),
+        (pltpu.VMEM((rows, width), bf16), pltpu.SemaphoreType.DMA((rows // LANES,))),
         HBM,
     )(powers, norm_gain.reshape(1, width), gated)
     return out
 
 
 def solution(mesh):
-    split = Mesh(mesh.devices.reshape(Y, Z, HEAD), ("y", "z", "head"))
-    seq = ("y", "z")
+    split = Mesh(mesh.devices.reshape(Y, FAR, NEAR, HEAD), ("y", "far", "near", "head"))
+    seq = ("y", "far", "near")
     placed = (
         P(seq, "head"),
         P(seq, "head"),

time: 85.8 us -> 83 us (0.967)
  waiting for transfers between devices: 4.89 us -> 11.6 us
  local copies, waits for them, and re-layouts: 7.71 us -> 1.34 us
  starting transfers between devices: 15.8 us -> 12.8 us
  blocking collectives: 48.6 us -> 47.4 us
  Pallas kernels: 8.29 us -> 9.39 us
    all_to_all x1, waiting for transfers between devices: 4.89 us -> 11.6 us  [local(): totals = lax.all_to_all(total, 'far', 0, 0, tiled=True)]
    unnamed x22 -> x8, local copies, waits for them, and re-layouts: 7.71 us -> 1.34 us
    all_to_all x1, starting transfers between devices: 15.8 us -> 12.8 us  [local(): totals = lax.all_to_all(total, 'far', 0, 0, tiled=True)]
    all_to_all x1, blocking collectives: 15.8 us -> 12.9 us  [local(): powers = lax.all_to_all(power, 'head', 0, 0, tiled=True)]
    all_to_all x2 -> x3, blocking collectives: 32.8 us -> 34.5 us  [the longest x1 12.9 us: local(): got = lax.all_to_all(piece, 'near', 0, 0, tiled=True)]
    pallas_call x1, Pallas kernels: 2.62 us -> 3.71 us  [local(): call(functools.partial(inner_kernel, heads, blocks), (((rows, width), f32...]
    pallas_call x4 -> x5, Pallas kernels: 5.11 us -> 5.12 us  [the longest x1 3.13 us: local(): call(functools.partial(summary_kernel, heads, blocks), (((NEAR, PIECE_ROW...]
  transfers between devices with their start and end apart: 1 -> 1, of which waited for: 1 -> 1; matrix products, arithmetic and copies ran while one was open for 0% -> 0% of each run, Pallas kernels for 3% -> 4%
where the time goes in v3:
time: 83 us; the launch traced here: 82.6 us
  blocking collectives  47.4 us (57%)
  starting transfers between devices  12.8 us (15%)
  waiting for transfers between devices  11.6 us (14%)
  Pallas kernels  9.39 us (11%)
  local copies, waits for them, and re-layouts  1.34 us (2%)
    all_to_all x1, blocking collectives, local(): got = lax.all_to_all(piece, 'near', 0, 0, tiled=True)  12.9 us
    all_to_all x1, blocking collectives, local(): powers = lax.all_to_all(power, 'head', 0, 0, tiled=True)  12.9 us
    all_to_all x1, starting transfers between devices, local(): totals = lax.all_to_all(total, 'far', 0, 0, tiled=True)  12.8 us
    all_to_all x1, blocking collectives, local(): entering = lax.all_to_all(joint, 'near', 0, 0, tiled=True)  12 us
    all_to_all x1, waiting for transfers between devices, local(): totals = lax.all_to_all(total, 'far', 0, 0, tiled=True)  11.6 us
    all_to_all x1, blocking collectives, local(): row_totals = lax.all_to_all(row_total, 'y', 0, 0, tiled=True)  9.6 us
    pallas_call x1, Pallas kernels, local(): call(functools.partial(inner_kernel, heads, blocks), (((rows, width), f32...  3.71 us
    pallas_call x1, Pallas kernels, local(): call(functools.partial(summary_kernel, heads, blocks), (((NEAR, PIECE_ROW...  3.13 us
  transfers between devices with their start and end apart: 1, of which 1 were waited for; matrix products, arithmetic and copies ran while one was open for 0% of the time, Pallas kernels for 4%

profile of v3, /device:TPU:1, one launch (start us, length us, event | category | flops | bytes accessed | tf_op | source)
XLA Modules:
  0.0 82.6 jit_solution(970401790928135567)
XLA Ops:
  0.0 3.1 %shard_map.82 = (f32[4,136,128]{2,1,0:T(8,128)S(1)}, f32[3,128,512]{2,1,0:T(8,128)S(1)}) custom-call(f32[4]{0:T(128)} %rate_hbm.3, s32[4,1024]{1,0:T(4,128)} %codes_hbm.3, bf16[1024,128]{1,0:T(8,128)(2,1)} %write_hbm.3, bf16[1024,512]{1,0:T(8,128)(2,1)} %x_hbm.3), custom_call_target="tpu_custom_call" | custom-call | flops 268435456 | bytes 3145728 | tf_op jit(solution)/shard_map/pallas_call | solution.py:306
  3.1 12.9 %all_to_all.25.got_ref = f32[4,136,128]{2,1,0:T(8,128)S(1)} all-to-all(f32[4,136,128]{2,1,0:T(8,128)S(1)} %get-tuple-element.23), channel_id=1, replica_groups=mesh['y'=4,'far'=4,'near'=4,'head'=8] {'near'}, dimensions={0} | all-to-all | bytes 557056 | tf_op jit(solution)/shard_map/all_to_all | solution.py:323
  16.0 0.7 shard_map.83
  16.8 12.8 %all-to-all-start.1 = ((f32[4,136,128]{2,1,0:T(8,128)}), f32[4,136,128]{2,1,0:T(8,128)S(1)}, u32[]{:S(2)}, u32[]{:S(2)}) async-start(f32[4,136,128]{2,1,0:T(8,128)} %get-tuple-element.25), calls=%async_computation.1 | async-start | bytes 557056 | tf_op jit(solution)/shard_map/all_to_all | solution.py:333
  29.6 3.7 %shard_map.84 = (f32[1024,512]{1,0:T(8,128)S(1)}, f32[1024,512]{1,0:T(8,128)S(1)}, f32[4,512]{1,0:T(4,128)S(1)}) custom-call(f32[4]{0:T(128)} %rate_hbm.3, f32[4]{0:T(128)} %skip_hbm.1, s32[4,1024]{1,0:T(4,128)} %codes_hbm.3, bf16[1024,128]{1,0:T(8,128)(2,1)} %write_hbm.3, bf16[1024,128]{1,0:T(8,128)(2,1)} %read_ref.1, bf16[1024,512]{1,0:T(8,128)(2,1)} %x_hbm.3, ...), custom_call_target="tpu_custom_call" | custom-call | flops 1073741824 | bytes 7340032 | tf_op jit(solution)/shard_map/pallas_call | solution.py:334
  33.4 0.0 copy-start
  33.4 1.3 %copy-done = f32[1024,512]{1,0:T(8,128)} copy-done((f32[1024,512]{1,0:T(8,128)}, f32[1024,512]{1,0:T(8,128)S(1)}, u32[]{:S(2)}) %copy-start) | copy-done | bytes 2097176
  34.7 11.6 %all-to-all-done.1.got_ref = f32[4,136,128]{2,1,0:T(8,128)S(1)} async-done(((f32[4,136,128]{2,1,0:T(8,128)}), f32[4,136,128]{2,1,0:T(8,128)S(1)}, u32[]{:S(2)}, u32[]{:S(2)}) %all-to-all-start.1) | async-done | bytes 278560 | tf_op jit(solution)/shard_map/all_to_all | solution.py:333
  46.4 9.6 %all_to_all.26.totals_ref = f32[4,136,128]{2,1,0:T(8,128)S(1)} all-to-all(f32[4,136,128]{2,1,0:T(8,128)S(1)} %get-tuple-element.31), channel_id=1, replica_groups=mesh['y'=4,'far'=4,'near'=4,'head'=8] {'y'}, dimensions={0} | all-to-all | bytes 557056 | tf_op jit(solution)/shard_map/all_to_all | solution.py:361
  56.0 0.0 copy-start.1
  56.0 0.0 copy-start.2
  56.0 0.1 shard_map.86
  56.0 12.0 %all_to_all.27.entering_ref = f32[4,128,128]{2,1,0:T(8,128)S(1)} all-to-all(f32[4,128,128]{2,1,0:T(8,128)S(1)} %shard_map.86), channel_id=1, replica_groups=mesh['y'=4,'far'=4,'near'=4,'head'=8] {'near'}, dimensions={0} | all-to-all | bytes 524288 | tf_op jit(solution)/shard_map/all_to_all | solution.py:365
  68.0 0.0 copy-done.1
  68.0 0.0 copy-done.2
  68.0 0.0 copy-start.3
  68.1 0.6 shard_map.87
  68.6 12.9 %all_to_all.28.power_ref = f32[8,8,128]{2,1,0:T(8,128)S(1)} all-to-all(f32[8,8,128]{2,1,0:T(8,128)S(1)} %get-tuple-element.39), channel_id=1, replica_groups=mesh['y'=4,'far'=4,'near'=4,'head'=8] {'head'}, dimensions={0} | all-to-all | bytes 65536 | tf_op jit(solution)/shard_map/all_to_all | solution.py:374
  81.5 0.0 copy-done.3
  81.5 1.2 %shard_map.88 = bf16[1024,512]{1,0:T(8,128)(2,1)} custom-call(f32[8,8,128]{2,1,0:T(8,128)S(1)} %all_to_all.28.power_ref, f32[1,512]{1,0:T(1,128)S(1)} %bitcast.1, f32[1024,512]{1,0:T(8,128)S(1)} %get-tuple-element.40.gated_ref), custom_call_target="tpu_custom_call" | custom-call | flops 1048576 | bytes 3145728 | tf_op jit(solution)/shard_map/pallas_call | solution.py:375
  (1 shorter events, 0.0 us)
Async XLA Ops:
  16.8 29.5 %all-to-all-start.1 = ((f32[4,136,128]{2,1,0:T(8,128)}), f32[4,136,128]{2,1,0:T(8,128)S(1)}, u32[]{:S(2)}, u32[]{:S(2)}) async-start(f32[4,136,128]{2,1,0:T(8,128)} %get-tuple-element.25), calls=%async_computation.1 | async-start | bytes 557056 | tf_op jit(solution)/shard_map/all_to_all | solution.py:333
  33.4 1.3 %copy-start = (f32[1024,512]{1,0:T(8,128)}, f32[1024,512]{1,0:T(8,128)S(1)}, u32[]{:S(2)}) copy-start(f32[1024,512]{1,0:T(8,128)S(1)} %get-tuple-element.38.factor_ref) | copy-start | bytes 6291460
  56.0 12.1 %copy-start.1 = (f32[1024,512]{1,0:T(8,128)S(1)}, f32[1024,512]{1,0:T(8,128)}, u32[]{:S(2)}) copy-start(f32[1024,512]{1,0:T(8,128)} %copy-done) | copy-start | bytes 6291460
  56.0 12.1 %copy-start.2 = (bf16[1024,128]{1,0:T(8,128)(2,1)S(1)}, bf16[1024,128]{1,0:T(8,128)(2,1)}, u32[]{:S(2)}) copy-start(bf16[1024,128]{1,0:T(8,128)(2,1)} %read_ref.1) | copy-start | bytes 786436
  68.0 13.4 %copy-start.3 = (f32[512]{0:T(512)S(1)}, f32[512]{0:T(512)}, u32[]{:S(2)}) copy-start(f32[512]{0:T(512)} %param.15) | copy-start | bytes 6148

commit v4 on v3

--- a/solution.py
+++ b/solution.py
@@ -67,6 +67,17 @@
     )
 
 
+def weighted_inputs(tail, x_ref, rows, k, heads):
+    return jnp.concatenate(
+        [
+            (tail[:, k * heads + h : k * heads + h + 1] * x_ref[rows, h * LANES : (h + 1) * LANES].astype(jnp.float32))
+            .astype(jnp.bfloat16)
+            for h in range(heads)
+        ],
+        axis=1,
+    )
+
+
 def summary_kernel(
     heads,
     blocks,
@@ -75,57 +86,34 @@
     write_hbm,
     x_hbm,
     piece_ref,
-    local_ref,
     rate_ref,
     codes_ref,
     write_ref,
     x_ref,
-    small_sem,
-    write_sem,
-    x_sem,
+    sem,
 ):
-    small = [
-        pltpu.make_async_copy(rate_hbm, rate_ref, small_sem.at[0]),
-        pltpu.make_async_copy(codes_hbm, codes_ref, small_sem.at[1]),
-    ]
-    parts_of = [pl.ds(k * GROUP, GROUP) for k in range(blocks)]
-    writes = [
-        pltpu.make_async_copy(write_hbm.at[rows], write_ref.at[rows], write_sem.at[k]) for k, rows in enumerate(parts_of)
-    ]
-    inputs = [pltpu.make_async_copy(x_hbm.at[rows], x_ref.at[rows], x_sem.at[k]) for k, rows in enumerate(parts_of)]
-    for copy in small:
+    pairs = ((rate_hbm, rate_ref), (codes_hbm, codes_ref), (write_hbm, write_ref), (x_hbm, x_ref))
+    copies = [pltpu.make_async_copy(a, b, sem.at[i]) for i, (a, b) in enumerate(pairs)]
+    for copy in copies:
         copy.start()
-    for k in range(blocks):
-        writes[k].start()
-        inputs[k].start()
     triangle = lower_triangle(GROUP).astype(jnp.float32).astype(jnp.bfloat16)
-    for copy in small:
+    for copy in copies[:2]:
         copy.wait()
     sums = code_columns(code_parts(codes_ref[...], heads, blocks), triangle)
     scale = exponent_row(rate_ref, heads, blocks)
     ends = sums[GROUP - 1 : GROUP, :]
-    tail = jnp.exp2((ends - sums) * scale)
-    block_decay = jnp.exp2(ends * scale)
+    to_end = [ends[:, (blocks - 1) * heads :]]
+    for k in range(blocks - 2, -1, -1):
+        to_end.insert(0, ends[:, k * heads : (k + 1) * heads] + to_end[0])
+    section_decay = jnp.exp2(to_end[0] * scale[:, :heads])
+    tail = jnp.exp2((jnp.concatenate(to_end, axis=1) - sums) * scale)
+    for copy in copies[2:]:
+        copy.wait()
     state = None
-    for k, rows in enumerate(parts_of):
-        writes[k].wait()
-        inputs[k].wait()
-        weighted = jnp.concatenate(
-            [
-                (tail[:, k * heads + h : k * heads + h + 1] * x_ref[rows, h * LANES : (h + 1) * LANES].astype(jnp.float32))
-                .astype(jnp.bfloat16)
-                for h in range(heads)
-            ],
-            axis=1,
-        )
-        added = matmul(write_ref[rows, :], weighted, TN)
-        if k:
-            local_ref[k - 1] = state
-            state = head_lanes(block_decay, k * heads, heads) * state + added
-        else:
-            state = added
-    total = sum(ends[:, k * heads : (k + 1) * heads] for k in range(blocks))
-    section_decay = jnp.exp2(total * scale[:, :heads])
+    for k in range(blocks):
+        rows = pl.ds(k * GROUP, GROUP)
+        added = matmul(write_ref[rows, :], weighted_inputs(tail, x_ref, rows, k, heads), TN)
+        state = state + added if k else added
     for h in range(heads):
         piece_ref[h, :STATE, :] = state[:, h * LANES : (h + 1) * LANES]
         piece_ref[h, STATE:, :] = jnp.broadcast_to(section_decay[:, h : h + 1], (PIECE_ROWS - STATE, LANES))
@@ -144,6 +132,7 @@
     base_ref,
     factor_ref,
     lead_ref,
+    local_ref,
     rate_ref,
     skip_ref,
     codes_ref,
@@ -169,6 +158,14 @@
     scale = exponent_row(rate_ref, heads, blocks)
     grown = jnp.exp2(columns * scale)
     ends = columns[GROUP - 1 : GROUP, :]
+    tail = jnp.exp2((ends - columns) * scale)
+    block_decay = jnp.exp2(ends * scale)
+    state = None
+    for k in range(blocks - 1):
+        rows = pl.ds(k * GROUP, GROUP)
+        added = matmul(write_ref[rows, :], weighted_inputs(tail, x_ref, rows, k, heads), TN)
+        state = head_lanes(block_decay, k * heads, heads) * state + added if k else added
+        local_ref[k] = state
     before = jnp.zeros((1, heads), jnp.float32)
     for k in range(blocks):
         lead_ref[k : k + 1, :] = head_lanes(jnp.exp2(before * scale[:, :heads]), 0, heads)
@@ -303,9 +300,9 @@
     heads = decay_rate.shape[0]
     blocks = rows // GROUP
     f32, bf16 = jnp.float32, jnp.bfloat16
-    piece, own = call(
+    (piece,) = call(
         functools.partial(summary_kernel, heads, blocks),
-        (((NEAR, PIECE_ROWS, LANES), f32), ((blocks - 1, LANES, width), f32)),
+        (((NEAR, PIECE_ROWS, LANES), f32),),
         [HBM] * 4,
         8 * MIB,
         1 << 28,
@@ -315,9 +312,7 @@
             pltpu.VMEM(decay_codes.shape, jnp.int32),
             pltpu.VMEM(write_proj.shape, bf16),
             pltpu.VMEM(ssm_input.shape, bf16),
-            pltpu.SemaphoreType.DMA((2,)),
-            pltpu.SemaphoreType.DMA((blocks,)),
-            pltpu.SemaphoreType.DMA((blocks,)),
+            pltpu.SemaphoreType.DMA((4,)),
         ),
     )(*in_hbm(decay_rate, decay_codes, write_proj, ssm_input))
     got = lax.all_to_all(piece, "near", 0, 0, tiled=True)
@@ -331,9 +326,9 @@
         MIB,
     )(got)
     totals = lax.all_to_all(total, "far", 0, 0, tiled=True)
-    base, factor, lead = call(
+    base, factor, lead, own = call(
         functools.partial(inner_kernel, heads, blocks),
-        (((rows, width), f32), ((rows, width), f32), ((blocks, width), f32)),
+        (((rows, width), f32), ((rows, width), f32), ((blocks, width), f32), ((blocks - 1, STATE, width), f32)),
         [HBM] * 7,
         16 * MIB,
         1 << 30,
@@ -349,7 +344,7 @@
             pltpu.SemaphoreType.DMA((7,)),
         ),
     )(*in_hbm(decay_rate, skip_gain, decay_codes, write_proj, read_proj, ssm_input, later_gate))
-    totals, base, factor, lead = lax.optimization_barrier((totals, base, factor, lead))
+    totals, base, factor, lead, own = lax.optimization_barrier((totals, base, factor, lead, own))
     group, row_total = call(
         far_kernel,
         (((PIECE_ROWS, LANES), f32), ((Y, PIECE_ROWS, LANES), f32)),

time: 83 us -> 82.2 us (level)
    pallas_call x1, Pallas kernels: 3.13 us -> 2.27 us  [local(): call(functools.partial(summary_kernel, heads, blocks), (((NEAR, PIECE_ROW...]
  transfers between devices with their start and end apart: 1 -> 1, of which waited for: 1 -> 1; matrix products, arithmetic and copies ran while one was open for 0% -> 0% of each run, Pallas kernels for 4% -> 5%
where the time goes in v4:
time: 82.2 us; the launch traced here: 81.8 us
  blocking collectives  47.4 us (58%)
  starting transfers between devices  12.8 us (16%)
  waiting for transfers between devices  10.9 us (13%)
  Pallas kernels  9.23 us (11%)
  local copies, waits for them, and re-layouts  1.34 us (2%)
    all_to_all x1, blocking collectives, local(): got = lax.all_to_all(piece, 'near', 0, 0, tiled=True)  12.9 us
    all_to_all x1, blocking collectives, local(): powers = lax.all_to_all(power, 'head', 0, 0, tiled=True)  12.9 us
    all_to_all x1, starting transfers between devices, local(): totals = lax.all_to_all(total, 'far', 0, 0, tiled=True)  12.8 us
    all_to_all x1, blocking collectives, local(): entering = lax.all_to_all(joint, 'near', 0, 0, tiled=True)  12 us
    all_to_all x1, waiting for transfers between devices, local(): totals = lax.all_to_all(total, 'far', 0, 0, tiled=True)  10.9 us
    all_to_all x1, blocking collectives, local(): row_totals = lax.all_to_all(row_total, 'y', 0, 0, tiled=True)  9.6 us
    pallas_call x1, Pallas kernels, local(): call(functools.partial(inner_kernel, heads, blocks), (((rows, width), f32...  4.4 us
    pallas_call x1, Pallas kernels, local(): call(functools.partial(summary_kernel, heads, blocks), (((NEAR, PIECE_ROW...  2.27 us
  transfers between devices with their start and end apart: 1, of which 1 were waited for; matrix products, arithmetic and copies ran while one was open for 0% of the time, Pallas kernels for 5%

profile of v4, /device:TPU:1, one launch (start us, length us, event | category | flops | bytes accessed | tf_op | source)
XLA Modules:
  0.0 81.8 jit_solution(19937309702279242)
XLA Ops:
  0.0 2.3 %shard_map.82 = f32[4,136,128]{2,1,0:T(8,128)S(1)} custom-call(f32[4]{0:T(128)} %rate_hbm.3, s32[4,1024]{1,0:T(4,128)} %codes_hbm.3, bf16[1024,128]{1,0:T(8,128)(2,1)} %write_hbm.3, bf16[1024,512]{1,0:T(8,128)(2,1)} %x_hbm.3), custom_call_target="tpu_custom_call" | custom-call | flops 268435456 | bytes 3145728 | tf_op jit(solution)/shard_map/pallas_call | solution.py:303
  2.3 12.9 %all_to_all.25.got_ref = f32[4,136,128]{2,1,0:T(8,128)S(1)} all-to-all(f32[4,136,128]{2,1,0:T(8,128)S(1)} %shard_map.82), channel_id=1, replica_groups=mesh['y'=4,'far'=4,'near'=4,'head'=8] {'near'}, dimensions={0} | all-to-all | bytes 557056 | tf_op jit(solution)/shard_map/all_to_all | solution.py:318
  15.2 0.7 shard_map.83
  15.9 12.8 %all-to-all-start.1 = ((f32[4,136,128]{2,1,0:T(8,128)}), f32[4,136,128]{2,1,0:T(8,128)S(1)}, u32[]{:S(2)}, u32[]{:S(2)}) async-start(f32[4,136,128]{2,1,0:T(8,128)} %get-tuple-element.24), calls=%async_computation.1 | async-start | bytes 557056 | tf_op jit(solution)/shard_map/all_to_all | solution.py:328
  28.8 4.4 %shard_map.84 = (f32[1024,512]{1,0:T(8,128)S(1)}, f32[1024,512]{1,0:T(8,128)S(1)}, f32[4,512]{1,0:T(4,128)S(1)}, f32[3,128,512]{2,1,0:T(8,128)S(1)}) custom-call(f32[4]{0:T(128)} %rate_hbm.3, f32[4]{0:T(128)} %skip_hbm.1, s32[4,1024]{1,0:T(4,128)} %codes_hbm.3, bf16[1024,128]{1,0:T(8,128)(2,1)} %write_hbm.3, bf16[1024,128]{1,0:T(8,128)(2,1)} %read_ref.1, ...), custom_call_target="tpu_custom_call" | custom-call | flops 1073741824 | bytes 7340032 | tf_op jit(solution)/shard_map/pallas_call | solution.py:329
  33.2 0.0 copy-start
  33.2 1.3 %copy-done = f32[1024,512]{1,0:T(8,128)} copy-done((f32[1024,512]{1,0:T(8,128)}, f32[1024,512]{1,0:T(8,128)S(1)}, u32[]{:S(2)}) %copy-start) | copy-done | bytes 2097176
  34.5 10.9 %all-to-all-done.1.got_ref = f32[4,136,128]{2,1,0:T(8,128)S(1)} async-done(((f32[4,136,128]{2,1,0:T(8,128)}), f32[4,136,128]{2,1,0:T(8,128)S(1)}, u32[]{:S(2)}, u32[]{:S(2)}) %all-to-all-start.1) | async-done | bytes 278560 | tf_op jit(solution)/shard_map/all_to_all | solution.py:328
  45.5 9.6 %all_to_all.26.totals_ref = f32[4,136,128]{2,1,0:T(8,128)S(1)} all-to-all(f32[4,136,128]{2,1,0:T(8,128)S(1)} %get-tuple-element.31), channel_id=1, replica_groups=mesh['y'=4,'far'=4,'near'=4,'head'=8] {'y'}, dimensions={0} | all-to-all | bytes 557056 | tf_op jit(solution)/shard_map/all_to_all | solution.py:356
  55.1 0.0 copy-start.1
  55.1 0.0 copy-start.2
  55.1 0.1 shard_map.86
  55.2 12.0 %all_to_all.27.entering_ref = f32[4,128,128]{2,1,0:T(8,128)S(1)} all-to-all(f32[4,128,128]{2,1,0:T(8,128)S(1)} %shard_map.86), channel_id=1, replica_groups=mesh['y'=4,'far'=4,'near'=4,'head'=8] {'near'}, dimensions={0} | all-to-all | bytes 524288 | tf_op jit(solution)/shard_map/all_to_all | solution.py:360
  67.2 0.0 copy-done.1
  67.2 0.0 copy-done.2
  67.2 0.0 copy-start.3
  67.2 0.6 shard_map.87
  67.8 12.9 %all_to_all.28.power_ref = f32[8,8,128]{2,1,0:T(8,128)S(1)} all-to-all(f32[8,8,128]{2,1,0:T(8,128)S(1)} %get-tuple-element.39), channel_id=1, replica_groups=mesh['y'=4,'far'=4,'near'=4,'head'=8] {'head'}, dimensions={0} | all-to-all | bytes 65536 | tf_op jit(solution)/shard_map/all_to_all | solution.py:369
  80.6 0.0 copy-done.3
  80.6 1.2 %shard_map.88 = bf16[1024,512]{1,0:T(8,128)(2,1)} custom-call(f32[8,8,128]{2,1,0:T(8,128)S(1)} %all_to_all.28.power_ref, f32[1,512]{1,0:T(1,128)S(1)} %bitcast.1, f32[1024,512]{1,0:T(8,128)S(1)} %get-tuple-element.40.gated_ref), custom_call_target="tpu_custom_call" | custom-call | flops 1048576 | bytes 3145728 | tf_op jit(solution)/shard_map/pallas_call | solution.py:370
  (1 shorter events, 0.0 us)
Async XLA Ops:
  15.9 29.5 %all-to-all-start.1 = ((f32[4,136,128]{2,1,0:T(8,128)}), f32[4,136,128]{2,1,0:T(8,128)S(1)}, u32[]{:S(2)}, u32[]{:S(2)}) async-start(f32[4,136,128]{2,1,0:T(8,128)} %get-tuple-element.24), calls=%async_computation.1 | async-start | bytes 557056 | tf_op jit(solution)/shard_map/all_to_all | solution.py:328
  33.2 1.3 %copy-start = (f32[1024,512]{1,0:T(8,128)}, f32[1024,512]{1,0:T(8,128)S(1)}, u32[]{:S(2)}) copy-start(f32[1024,512]{1,0:T(8,128)S(1)} %get-tuple-element.38.factor_ref) | copy-start | bytes 6291460
  55.1 12.1 %copy-start.1 = (f32[1024,512]{1,0:T(8,128)S(1)}, f32[1024,512]{1,0:T(8,128)}, u32[]{:S(2)}) copy-start(f32[1024,512]{1,0:T(8,128)} %copy-done) | copy-start | bytes 6291460
  55.1 12.1 %copy-start.2 = (bf16[1024,128]{1,0:T(8,128)(2,1)S(1)}, bf16[1024,128]{1,0:T(8,128)(2,1)}, u32[]{:S(2)}) copy-start(bf16[1024,128]{1,0:T(8,128)(2,1)} %read_ref.1) | copy-start | bytes 786436
  67.2 13.4 %copy-start.3 = (f32[512]{0:T(512)S(1)}, f32[512]{0:T(512)}, u32[]{:S(2)}) copy-start(f32[512]{0:T(512)} %param.15) | copy-start | bytes 6148

commit v5 on v4

--- a/solution.py
+++ b/solution.py
@@ -102,18 +102,17 @@
     sums = code_columns(code_parts(codes_ref[...], heads, blocks), triangle)
     scale = exponent_row(rate_ref, heads, blocks)
     ends = sums[GROUP - 1 : GROUP, :]
-    to_end = [ends[:, (blocks - 1) * heads :]]
-    for k in range(blocks - 2, -1, -1):
-        to_end.insert(0, ends[:, k * heads : (k + 1) * heads] + to_end[0])
-    section_decay = jnp.exp2(to_end[0] * scale[:, :heads])
-    tail = jnp.exp2((jnp.concatenate(to_end, axis=1) - sums) * scale)
+    tail = jnp.exp2((ends - sums) * scale)
+    block_decay = jnp.exp2(ends * scale)
+    total = sum(ends[:, k * heads : (k + 1) * heads] for k in range(blocks))
+    section_decay = jnp.exp2(total * scale[:, :heads])
     for copy in copies[2:]:
         copy.wait()
     state = None
     for k in range(blocks):
         rows = pl.ds(k * GROUP, GROUP)
         added = matmul(write_ref[rows, :], weighted_inputs(tail, x_ref, rows, k, heads), TN)
-        state = state + added if k else added
+        state = head_lanes(block_decay, k * heads, heads) * state + added if k else added
     for h in range(heads):
         piece_ref[h, :STATE, :] = state[:, h * LANES : (h + 1) * LANES]
         piece_ref[h, STATE:, :] = jnp.broadcast_to(section_decay[:, h : h + 1], (PIECE_ROWS - STATE, LANES))

time: 82.2 us -> 82.2 us (level)
  no operation moved by 1% of the time
where the time goes in v5:
time: 82.2 us; the launch traced here: 81.8 us
  blocking collectives  47.4 us (58%)
  starting transfers between devices  12.8 us (16%)
  waiting for transfers between devices  10.9 us (13%)
  Pallas kernels  9.25 us (11%)
  local copies, waits for them, and re-layouts  1.34 us (2%)
    all_to_all x1, blocking collectives, local(): got = lax.all_to_all(piece, 'near', 0, 0, tiled=True)  12.9 us
    all_to_all x1, blocking collectives, local(): powers = lax.all_to_all(power, 'head', 0, 0, tiled=True)  12.9 us
    all_to_all x1, starting transfers between devices, local(): totals = lax.all_to_all(total, 'far', 0, 0, tiled=True)  12.8 us
    all_to_all x1, blocking collectives, local(): entering = lax.all_to_all(joint, 'near', 0, 0, tiled=True)  12 us
    all_to_all x1, waiting for transfers between devices, local(): totals = lax.all_to_all(total, 'far', 0, 0, tiled=True)  10.9 us
    all_to_all x1, blocking collectives, local(): row_totals = lax.all_to_all(row_total, 'y', 0, 0, tiled=True)  9.6 us
    pallas_call x1, Pallas kernels, local(): call(functools.partial(inner_kernel, heads, blocks), (((rows, width), f32...  4.41 us
    pallas_call x1, Pallas kernels, local(): call(functools.partial(summary_kernel, heads, blocks), (((NEAR, PIECE_ROW...  2.29 us
  transfers between devices with their start and end apart: 1, of which 1 were waited for; matrix products, arithmetic and copies ran while one was open for 0% of the time, Pallas kernels for 5%

profile of v5, /device:TPU:1, one launch (start us, length us, event | category | flops | bytes accessed | tf_op | source)
XLA Modules:
  0.0 81.8 jit_solution(13127945126049271809)
XLA Ops:
  0.0 2.3 %shard_map.82 = f32[4,136,128]{2,1,0:T(8,128)S(1)} custom-call(f32[4]{0:T(128)} %rate_hbm.3, s32[4,1024]{1,0:T(4,128)} %codes_hbm.3, bf16[1024,128]{1,0:T(8,128)(2,1)} %write_hbm.3, bf16[1024,512]{1,0:T(8,128)(2,1)} %x_hbm.3), custom_call_target="tpu_custom_call" | custom-call | flops 268435456 | bytes 3145728 | tf_op jit(solution)/shard_map/pallas_call | solution.py:302
  2.3 12.9 %all_to_all.25.got_ref = f32[4,136,128]{2,1,0:T(8,128)S(1)} all-to-all(f32[4,136,128]{2,1,0:T(8,128)S(1)} %shard_map.82), channel_id=1, replica_groups=mesh['y'=4,'far'=4,'near'=4,'head'=8] {'near'}, dimensions={0} | all-to-all | bytes 557056 | tf_op jit(solution)/shard_map/all_to_all | solution.py:317
  15.2 0.7 shard_map.83
  16.0 12.8 %all-to-all-start.1 = ((f32[4,136,128]{2,1,0:T(8,128)}), f32[4,136,128]{2,1,0:T(8,128)S(1)}, u32[]{:S(2)}, u32[]{:S(2)}) async-start(f32[4,136,128]{2,1,0:T(8,128)} %get-tuple-element.24), calls=%async_computation.1 | async-start | bytes 557056 | tf_op jit(solution)/shard_map/all_to_all | solution.py:327
  28.8 4.4 %shard_map.84 = (f32[1024,512]{1,0:T(8,128)S(1)}, f32[1024,512]{1,0:T(8,128)S(1)}, f32[4,512]{1,0:T(4,128)S(1)}, f32[3,128,512]{2,1,0:T(8,128)S(1)}) custom-call(f32[4]{0:T(128)} %rate_hbm.3, f32[4]{0:T(128)} %skip_hbm.1, s32[4,1024]{1,0:T(4,128)} %codes_hbm.3, bf16[1024,128]{1,0:T(8,128)(2,1)} %write_hbm.3, bf16[1024,128]{1,0:T(8,128)(2,1)} %read_ref.1, ...), custom_call_target="tpu_custom_call" | custom-call | flops 1073741824 | bytes 7340032 | tf_op jit(solution)/shard_map/pallas_call | solution.py:328
  33.2 0.0 copy-start
  33.2 1.3 %copy-done = f32[1024,512]{1,0:T(8,128)} copy-done((f32[1024,512]{1,0:T(8,128)}, f32[1024,512]{1,0:T(8,128)S(1)}, u32[]{:S(2)}) %copy-start) | copy-done | bytes 2097176
  34.6 10.9 %all-to-all-done.1.got_ref = f32[4,136,128]{2,1,0:T(8,128)S(1)} async-done(((f32[4,136,128]{2,1,0:T(8,128)}), f32[4,136,128]{2,1,0:T(8,128)S(1)}, u32[]{:S(2)}, u32[]{:S(2)}) %all-to-all-start.1) | async-done | bytes 278560 | tf_op jit(solution)/shard_map/all_to_all | solution.py:327
  45.5 9.6 %all_to_all.26.totals_ref = f32[4,136,128]{2,1,0:T(8,128)S(1)} all-to-all(f32[4,136,128]{2,1,0:T(8,128)S(1)} %get-tuple-element.31), channel_id=1, replica_groups=mesh['y'=4,'far'=4,'near'=4,'head'=8] {'y'}, dimensions={0} | all-to-all | bytes 557056 | tf_op jit(solution)/shard_map/all_to_all | solution.py:355
  55.1 0.0 copy-start.1
  55.1 0.0 copy-start.2
  55.1 0.1 shard_map.86
  55.2 12.0 %all_to_all.27.entering_ref = f32[4,128,128]{2,1,0:T(8,128)S(1)} all-to-all(f32[4,128,128]{2,1,0:T(8,128)S(1)} %shard_map.86), channel_id=1, replica_groups=mesh['y'=4,'far'=4,'near'=4,'head'=8] {'near'}, dimensions={0} | all-to-all | bytes 524288 | tf_op jit(solution)/shard_map/all_to_all | solution.py:359
  67.2 0.0 copy-done.1
  67.2 0.0 copy-done.2
  67.2 0.0 copy-start.3
  67.2 0.6 shard_map.87
  67.8 12.9 %all_to_all.28.power_ref = f32[8,8,128]{2,1,0:T(8,128)S(1)} all-to-all(f32[8,8,128]{2,1,0:T(8,128)S(1)} %get-tuple-element.39), channel_id=1, replica_groups=mesh['y'=4,'far'=4,'near'=4,'head'=8] {'head'}, dimensions={0} | all-to-all | bytes 65536 | tf_op jit(solution)/shard_map/all_to_all | solution.py:368
  80.6 0.0 copy-done.3
  80.6 1.2 %shard_map.88 = bf16[1024,512]{1,0:T(8,128)(2,1)} custom-call(f32[8,8,128]{2,1,0:T(8,128)S(1)} %all_to_all.28.power_ref, f32[1,512]{1,0:T(1,128)S(1)} %bitcast.1, f32[1024,512]{1,0:T(8,128)S(1)} %get-tuple-element.40.gated_ref), custom_call_target="tpu_custom_call" | custom-call | flops 1048576 | bytes 3145728 | tf_op jit(solution)/shard_map/pallas_call | solution.py:369
  (1 shorter events, 0.0 us)
Async XLA Ops:
  16.0 29.5 %all-to-all-start.1 = ((f32[4,136,128]{2,1,0:T(8,128)}), f32[4,136,128]{2,1,0:T(8,128)S(1)}, u32[]{:S(2)}, u32[]{:S(2)}) async-start(f32[4,136,128]{2,1,0:T(8,128)} %get-tuple-element.24), calls=%async_computation.1 | async-start | bytes 557056 | tf_op jit(solution)/shard_map/all_to_all | solution.py:327
  33.2 1.3 %copy-start = (f32[1024,512]{1,0:T(8,128)}, f32[1024,512]{1,0:T(8,128)S(1)}, u32[]{:S(2)}) copy-start(f32[1024,512]{1,0:T(8,128)S(1)} %get-tuple-element.38.factor_ref) | copy-start | bytes 6291460
  55.1 12.1 %copy-start.1 = (f32[1024,512]{1,0:T(8,128)S(1)}, f32[1024,512]{1,0:T(8,128)}, u32[]{:S(2)}) copy-start(f32[1024,512]{1,0:T(8,128)} %copy-done) | copy-start | bytes 6291460
  55.1 12.1 %copy-start.2 = (bf16[1024,128]{1,0:T(8,128)(2,1)S(1)}, bf16[1024,128]{1,0:T(8,128)(2,1)}, u32[]{:S(2)}) copy-start(bf16[1024,128]{1,0:T(8,128)(2,1)} %read_ref.1) | copy-start | bytes 786436
  67.2 13.4 %copy-start.3 = (f32[512]{0:T(512)S(1)}, f32[512]{0:T(512)}, u32[]{:S(2)}) copy-start(f32[512]{0:T(512)} %param.15) | copy-start | bytes 6148

commit v6 on v5

--- a/solution.py
+++ b/solution.py
@@ -17,7 +17,10 @@
 EPS = 1e-05
 Y, FAR, NEAR, HEAD = 4, 4, 4, 8
 STATE = 128
-PIECE_ROWS = 136
+OWNERS = Y * NEAR
+PIECE = 32
+PIECE_ROWS = 40
+TOTAL_ROWS = Y * PIECE + 8
 MIB = 1 << 20
 NT = (((1,), (1,)), ((), ()))
 TN = (((0,), (0,)), ((), ()))
@@ -113,9 +116,12 @@
         rows = pl.ds(k * GROUP, GROUP)
         added = matmul(write_ref[rows, :], weighted_inputs(tail, x_ref, rows, k, heads), TN)
         state = head_lanes(block_decay, k * heads, heads) * state + added if k else added
+    quarters = STATE // PIECE
     for h in range(heads):
-        piece_ref[h, :STATE, :] = state[:, h * LANES : (h + 1) * LANES]
-        piece_ref[h, STATE:, :] = jnp.broadcast_to(section_decay[:, h : h + 1], (PIECE_ROWS - STATE, LANES))
+        decay = jnp.broadcast_to(section_decay[:, h : h + 1], (PIECE_ROWS - PIECE, LANES))
+        for q in range(quarters):
+            piece_ref[h * quarters + q, :PIECE, :] = state[q * PIECE : (q + 1) * PIECE, h * LANES : (h + 1) * LANES]
+            piece_ref[h * quarters + q, PIECE:, :] = decay
 
 
 def inner_kernel(
@@ -198,49 +204,48 @@
 
 
 def near_kernel(got_ref, prefix_ref, decay_ref, total_ref):
-    state = jnp.zeros((STATE, LANES), jnp.float32)
-    decay = jnp.ones((PIECE_ROWS - STATE, LANES), jnp.float32)
-    for i in range(NEAR):
-        prefix_ref[i] = state
-        decay_ref[i] = decay
-        step = got_ref[i, STATE:, :]
-        state = step[:1] * state + got_ref[i, :STATE, :]
-        decay = step * decay
+    place = lax.broadcasted_iota(jnp.int32, (TOTAL_ROWS - Y * PIECE, LANES), 0)
+    decays = jnp.zeros((TOTAL_ROWS - Y * PIECE, LANES), jnp.float32)
+    totals = []
+    for y in range(Y):
+        state = jnp.zeros((PIECE, LANES), jnp.float32)
+        decay = jnp.ones((PIECE_ROWS - PIECE, LANES), jnp.float32)
+        for i in range(y * NEAR, (y + 1) * NEAR):
+            prefix_ref[i] = state
+            decay_ref[i] = decay
+            step = got_ref[i, PIECE:, :]
+            state = step[:1] * state + got_ref[i, :PIECE, :]
+            decay = step * decay
+        totals.append(state)
+        decays = jnp.where(place == y, decay, decays)
     for j in range(FAR):
-        total_ref[j, :STATE, :] = state
-        total_ref[j, STATE:, :] = decay
-
-
-def far_kernel(got_ref, prefix_ref, total_ref):
+        for y in range(Y):
+            total_ref[j, y * PIECE : (y + 1) * PIECE, :] = totals[y]
+        total_ref[j, Y * PIECE :, :] = decays
+
+
+def join_kernel(got_ref, prefix_ref, decay_ref, out_ref):
     mine = lax.axis_index("far")
-    state = jnp.zeros((STATE, LANES), jnp.float32)
-    decay = jnp.ones((PIECE_ROWS - STATE, LANES), jnp.float32)
-    own, own_decay = state, decay
-    for i in range(FAR):
-        own = jnp.where(i == mine, state, own)
-        own_decay = jnp.where(i == mine, decay, own_decay)
-        step = got_ref[i, STATE:, :]
-        state = step[:1] * state + got_ref[i, :STATE, :]
-        decay = step * decay
-    prefix_ref[:STATE, :] = own
-    prefix_ref[STATE:, :] = own_decay
-    for j in range(Y):
-        total_ref[j, :STATE, :] = state
-        total_ref[j, STATE:, :] = decay
-
-
-def join_kernel(totals_ref, group_ref, prefix_ref, decay_ref, out_ref):
-    mine = lax.axis_index("y")
-    state = jnp.zeros((STATE, LANES), jnp.float32)
-    for j in range(Y - 1):
-        state = jnp.where(j < mine, totals_ref[j, STATE : STATE + 1, :] * state + totals_ref[j, :STATE, :], state)
-    state = group_ref[STATE : STATE + 1, :] * state + group_ref[:STATE, :]
-    for i in range(NEAR):
-        out_ref[i] = decay_ref[i, :1, :] * state + prefix_ref[i]
+    state = jnp.zeros((PIECE, LANES), jnp.float32)
+    for y in range(Y):
+        own = state
+        for i in range(FAR):
+            own = jnp.where(i == mine, state, own)
+            decay = got_ref[i, Y * PIECE + y : Y * PIECE + y + 1, :]
+            state = decay * state + got_ref[i, y * PIECE : (y + 1) * PIECE, :]
+        for i in range(y * NEAR, (y + 1) * NEAR):
+            out_ref[i] = decay_ref[i, :1, :] * own + prefix_ref[i]
 
 
 def carry_kernel(heads, blocks, entering_ref, local_ref, lead_ref, read_ref, base_ref, factor_ref, gated_ref, power_ref):
-    entering = jnp.concatenate([entering_ref[h] for h in range(heads)], axis=1)
+    quarters = STATE // PIECE
+    entering = jnp.concatenate(
+        [
+            jnp.concatenate([entering_ref[h * quarters + q] for q in range(quarters)], axis=0)
+            for h in range(heads)
+        ],
+        axis=1,
+    )
     sums = []
     for k in range(blocks):
         rows = pl.ds(k * GROUP, GROUP)
@@ -301,7 +306,7 @@
     f32, bf16 = jnp.float32, jnp.bfloat16
     (piece,) = call(
         functools.partial(summary_kernel, heads, blocks),
-        (((NEAR, PIECE_ROWS, LANES), f32),),
+        (((OWNERS, PIECE_ROWS, LANES), f32),),
         [HBM] * 4,
         8 * MIB,
         1 << 28,
@@ -314,11 +319,11 @@
             pltpu.SemaphoreType.DMA((4,)),
         ),
     )(*in_hbm(decay_rate, decay_codes, write_proj, ssm_input))
-    got = lax.all_to_all(piece, "near", 0, 0, tiled=True)
+    got = lax.all_to_all(piece, ("y", "near"), 0, 0, tiled=True)
     got, later_gate = lax.optimization_barrier((got, gate_input))
     prefix, prefix_decay, total = call(
         near_kernel,
-        (((NEAR, STATE, LANES), f32), ((NEAR, PIECE_ROWS - STATE, LANES), f32), ((FAR, PIECE_ROWS, LANES), f32)),
+        (((OWNERS, PIECE, LANES), f32), ((OWNERS, PIECE_ROWS - PIECE, LANES), f32), ((FAR, TOTAL_ROWS, LANES), f32)),
         [VMEM],
         8 * MIB,
         1 << 20,
@@ -344,19 +349,10 @@
         ),
     )(*in_hbm(decay_rate, skip_gain, decay_codes, write_proj, read_proj, ssm_input, later_gate))
     totals, base, factor, lead, own = lax.optimization_barrier((totals, base, factor, lead, own))
-    group, row_total = call(
-        far_kernel,
-        (((PIECE_ROWS, LANES), f32), ((Y, PIECE_ROWS, LANES), f32)),
-        [VMEM],
-        8 * MIB,
-        1 << 33,
-        MIB,
-    )(totals)
-    row_totals = lax.all_to_all(row_total, "y", 0, 0, tiled=True)
-    (joint,) = call(join_kernel, (((NEAR, STATE, LANES), f32),), [VMEM] * 4, 8 * MIB, 1 << 33, MIB)(
-        row_totals, group, prefix, prefix_decay
-    )
-    entering = lax.all_to_all(joint, "near", 0, 0, tiled=True)
+    (joint,) = call(join_kernel, (((OWNERS, PIECE, LANES), f32),), [VMEM] * 3, 8 * MIB, 1 << 33, MIB)(
+        totals, prefix, prefix_decay
+    )
+    entering = lax.all_to_all(joint, ("y", "near"), 0, 0, tiled=True)
     gated, power = call(
         functools.partial(carry_kernel, heads, blocks),
         (((rows, width), f32), ((HEAD, rows // LANES, LANES), f32)),

time: 82.2 us -> 79.8 us (0.971)
  waiting for transfers between devices: 10.9 us -> 9.91 us
    all_to_all x3 -> x2, blocking collectives: 34.5 us -> 33.2 us  [the longest x1 20.3 us: local(): got = lax.all_to_all(piece, ('y', 'near'), 0, 0, tiled=True)]
    all_to_all x1, waiting for transfers between devices: 10.9 us -> 9.91 us  [local(): totals = lax.all_to_all(total, 'far', 0, 0, tiled=True)]
    all_to_all x1, blocking collectives: 12.9 us -> 13.7 us  [local(): powers = lax.all_to_all(power, 'head', 0, 0, tiled=True)]
    pallas_call x4 -> x3, Pallas kernels: 3.13 us -> 3.1 us  [the longest x1 2.29 us: local(): call(functools.partial(summary_kernel, heads, blocks), (((OWNERS, PIECE_R...]
  transfers between devices with their start and end apart: 1 -> 1, of which waited for: 1 -> 1; matrix products, arithmetic and copies ran while one was open for 0% -> 0% of each run, Pallas kernels for 5% -> 6%
where the time goes in v6:
time: 79.8 us; the launch traced here: 79.5 us
  blocking collectives  46.9 us (59%)
  starting transfers between devices  12.1 us (15%)
  waiting for transfers between devices  9.91 us (12%)
  Pallas kernels  9.22 us (12%)
  local copies, waits for them, and re-layouts  1.35 us (2%)
    all_to_all x1, blocking collectives, local(): got = lax.all_to_all(piece, ('y', 'near'), 0, 0, tiled=True)  20.3 us
    all_to_all x1, blocking collectives, local(): powers = lax.all_to_all(power, 'head', 0, 0, tiled=True)  13.7 us
    all_to_all x1, blocking collectives, local(): entering = lax.all_to_all(joint, ('y', 'near'), 0, 0, tiled=True)  12.9 us
    all_to_all x1, starting transfers between devices, local(): totals = lax.all_to_all(total, 'far', 0, 0, tiled=True)  12.1 us
    all_to_all x1, waiting for transfers between devices, local(): totals = lax.all_to_all(total, 'far', 0, 0, tiled=True)  9.91 us
    pallas_call x1, Pallas kernels, local(): call(functools.partial(inner_kernel, heads, blocks), (((rows, width), f32...  4.4 us
    pallas_call x1, Pallas kernels, local(): call(functools.partial(summary_kernel, heads, blocks), (((OWNERS, PIECE_R...  2.29 us
  transfers between devices with their start and end apart: 1, of which 1 were waited for; matrix products, arithmetic and copies ran while one was open for 0% of the time, Pallas kernels for 6%

profile of v6, /device:TPU:1, one launch (start us, length us, event | category | flops | bytes accessed | tf_op | source)
XLA Modules:
  0.0 79.5 jit_solution(17066320807793922733)
XLA Ops:
  0.0 2.3 %shard_map.82 = f32[16,40,128]{2,1,0:T(8,128)S(1)} custom-call(f32[4]{0:T(128)} %rate_hbm.3, s32[4,1024]{1,0:T(4,128)} %codes_hbm.3, bf16[1024,128]{1,0:T(8,128)(2,1)} %write_hbm.3, bf16[1024,512]{1,0:T(8,128)(2,1)} %x_hbm.3), custom_call_target="tpu_custom_call" | custom-call | flops 268435456 | bytes 3145728 | tf_op jit(solution)/shard_map/pallas_call | solution.py:307
  2.3 20.3 %all_to_all.20.got_ref = f32[16,40,128]{2,1,0:T(8,128)S(1)} all-to-all(f32[16,40,128]{2,1,0:T(8,128)S(1)} %shard_map.82), channel_id=1, replica_groups=mesh['y'=4,'far'=4,'near'=4,'head'=8] {'y','near'}, dimensions={0} | all-to-all | bytes 655360 | tf_op jit(solution)/shard_map/all_to_all | solution.py:322
  22.6 0.7 shard_map.83
  23.3 12.1 %all-to-all-start.1 = ((f32[4,136,128]{2,1,0:T(8,128)}), f32[4,136,128]{2,1,0:T(8,128)S(1)}, u32[]{:S(2)}, u32[]{:S(2)}) async-start(f32[4,136,128]{2,1,0:T(8,128)} %get-tuple-element.22), calls=%async_computation.1 | async-start | bytes 557056 | tf_op jit(solution)/shard_map/all_to_all | solution.py:332
  35.4 4.4 %shard_map.84 = (f32[1024,512]{1,0:T(8,128)S(1)}, f32[1024,512]{1,0:T(8,128)S(1)}, f32[4,512]{1,0:T(4,128)S(1)}, f32[3,128,512]{2,1,0:T(8,128)S(1)}) custom-call(f32[4]{0:T(128)} %rate_hbm.3, f32[4]{0:T(128)} %skip_hbm.1, s32[4,1024]{1,0:T(4,128)} %codes_hbm.3, bf16[1024,128]{1,0:T(8,128)(2,1)} %write_hbm.3, bf16[1024,128]{1,0:T(8,128)(2,1)} %read_ref.1, ...), custom_call_target="tpu_custom_call" | custom-call | flops 1073741824 | bytes 7340032 | tf_op jit(solution)/shard_map/pallas_call | solution.py:333
  39.8 0.0 copy-start
  39.8 1.3 %copy-done = f32[1024,512]{1,0:T(8,128)} copy-done((f32[1024,512]{1,0:T(8,128)}, f32[1024,512]{1,0:T(8,128)S(1)}, u32[]{:S(2)}) %copy-start) | copy-done | bytes 2097176
  41.2 9.9 %all-to-all-done.1.got_ref = f32[4,136,128]{2,1,0:T(8,128)S(1)} async-done(((f32[4,136,128]{2,1,0:T(8,128)}), f32[4,136,128]{2,1,0:T(8,128)S(1)}, u32[]{:S(2)}, u32[]{:S(2)}) %all-to-all-start.1) | async-done | bytes 278560 | tf_op jit(solution)/shard_map/all_to_all | solution.py:332
  51.1 0.0 copy-start.1
  51.1 0.0 copy-start.2
  51.1 0.1 shard_map.85
  51.2 12.9 %all_to_all.21.entering_ref = f32[16,32,128]{2,1,0:T(8,128)S(1)} all-to-all(f32[16,32,128]{2,1,0:T(8,128)S(1)} %shard_map.85), channel_id=1, replica_groups=mesh['y'=4,'far'=4,'near'=4,'head'=8] {'y','near'}, dimensions={0} | all-to-all | bytes 524288 | tf_op jit(solution)/shard_map/all_to_all | solution.py:355
  64.1 0.0 copy-done.1
  64.1 0.0 copy-done.2
  64.1 0.0 copy-start.3
  64.1 0.6 shard_map.86
  64.6 13.7 %all_to_all.22.power_ref = f32[8,8,128]{2,1,0:T(8,128)S(1)} all-to-all(f32[8,8,128]{2,1,0:T(8,128)S(1)} %get-tuple-element.35), channel_id=1, replica_groups=mesh['y'=4,'far'=4,'near'=4,'head'=8] {'head'}, dimensions={0} | all-to-all | bytes 65536 | tf_op jit(solution)/shard_map/all_to_all | solution.py:364
  78.3 0.0 copy-done.3
  78.3 1.2 %shard_map.87 = bf16[1024,512]{1,0:T(8,128)(2,1)} custom-call(f32[8,8,128]{2,1,0:T(8,128)S(1)} %all_to_all.22.power_ref, f32[1,512]{1,0:T(1,128)S(1)} %bitcast.1, f32[1024,512]{1,0:T(8,128)S(1)} %get-tuple-element.36.gated_ref), custom_call_target="tpu_custom_call" | custom-call | flops 1048576 | bytes 3145728 | tf_op jit(solution)/shard_map/pallas_call | solution.py:365
Async XLA Ops:
  23.3 27.8 %all-to-all-start.1 = ((f32[4,136,128]{2,1,0:T(8,128)}), f32[4,136,128]{2,1,0:T(8,128)S(1)}, u32[]{:S(2)}, u32[]{:S(2)}) async-start(f32[4,136,128]{2,1,0:T(8,128)} %get-tuple-element.22), calls=%async_computation.1 | async-start | bytes 557056 | tf_op jit(solution)/shard_map/all_to_all | solution.py:332
  39.8 1.3 %copy-start = (f32[1024,512]{1,0:T(8,128)}, f32[1024,512]{1,0:T(8,128)S(1)}, u32[]{:S(2)}) copy-start(f32[1024,512]{1,0:T(8,128)S(1)} %get-tuple-element.34.factor_ref) | copy-start | bytes 6291460
  51.1 13.0 %copy-start.1 = (f32[1024,512]{1,0:T(8,128)S(1)}, f32[1024,512]{1,0:T(8,128)}, u32[]{:S(2)}) copy-start(f32[1024,512]{1,0:T(8,128)} %copy-done) | copy-start | bytes 6291460
  51.1 13.0 %copy-start.2 = (bf16[1024,128]{1,0:T(8,128)(2,1)S(1)}, bf16[1024,128]{1,0:T(8,128)(2,1)}, u32[]{:S(2)}) copy-start(bf16[1024,128]{1,0:T(8,128)(2,1)} %read_ref.1) | copy-start | bytes 786436
  64.1 14.3 %copy-start.3 = (f32[512]{0:T(512)S(1)}, f32[512]{0:T(512)}, u32[]{:S(2)}) copy-start(f32[512]{0:T(512)} %param.15) | copy-start | bytes 6148

commit v7 on v6

--- a/solution.py
+++ b/solution.py
@@ -218,10 +218,9 @@
             decay = step * decay
         totals.append(state)
         decays = jnp.where(place == y, decay, decays)
-    for j in range(FAR):
-        for y in range(Y):
-            total_ref[j, y * PIECE : (y + 1) * PIECE, :] = totals[y]
-        total_ref[j, Y * PIECE :, :] = decays
+    for y in range(Y):
+        total_ref[y * PIECE : (y + 1) * PIECE, :] = totals[y]
+    total_ref[Y * PIECE :, :] = decays
 
 
 def join_kernel(got_ref, prefix_ref, decay_ref, out_ref):
@@ -320,16 +319,6 @@
         ),
     )(*in_hbm(decay_rate, decay_codes, write_proj, ssm_input))
     got = lax.all_to_all(piece, ("y", "near"), 0, 0, tiled=True)
-    got, later_gate = lax.optimization_barrier((got, gate_input))
-    prefix, prefix_decay, total = call(
-        near_kernel,
-        (((OWNERS, PIECE, LANES), f32), ((OWNERS, PIECE_ROWS - PIECE, LANES), f32), ((FAR, TOTAL_ROWS, LANES), f32)),
-        [VMEM],
-        8 * MIB,
-        1 << 20,
-        MIB,
-    )(got)
-    totals = lax.all_to_all(total, "far", 0, 0, tiled=True)
     base, factor, lead, own = call(
         functools.partial(inner_kernel, heads, blocks),
         (((rows, width), f32), ((rows, width), f32), ((blocks, width), f32), ((blocks - 1, STATE, width), f32)),
@@ -347,8 +336,17 @@
             pltpu.VMEM(gate_input.shape, bf16),
             pltpu.SemaphoreType.DMA((7,)),
         ),
-    )(*in_hbm(decay_rate, skip_gain, decay_codes, write_proj, read_proj, ssm_input, later_gate))
-    totals, base, factor, lead, own = lax.optimization_barrier((totals, base, factor, lead, own))
+    )(*in_hbm(decay_rate, skip_gain, decay_codes, write_proj, read_proj, ssm_input, gate_input))
+    got, base, factor, lead, own = lax.optimization_barrier((got, base, factor, lead, own))
+    prefix, prefix_decay, total = call(
+        near_kernel,
+        (((OWNERS, PIECE, LANES), f32), ((OWNERS, PIECE_ROWS - PIECE, LANES), f32), ((TOTAL_ROWS, LANES), f32)),
+        [VMEM],
+        8 * MIB,
+        1 << 33,
+        MIB,
+    )(got)
+    totals = lax.all_gather(total, "far")
     (joint,) = call(join_kernel, (((OWNERS, PIECE, LANES), f32),), [VMEM] * 3, 8 * MIB, 1 << 33, MIB)(
         totals, prefix, prefix_decay
     )

time: 79.8 us -> 74.6 us (0.935)
  waiting for transfers between devices: 9.91 us -> 5.5 us
  starting transfers between devices: 12.1 us -> 9.2 us
  blocking collectives: 46.9 us -> 48.9 us
    all_gather x0 -> x1, blocking collectives: none -> 23.3 us  [local(): totals = lax.all_gather(total, 'far')]
    all_to_all x1 -> x0, blocking collectives: 20.3 us -> none  [local(): got = lax.all_to_all(piece, ('y', 'near'), 0, 0, tiled=True)]
    all_to_all x1, waiting for transfers between devices: 9.91 us -> 5.5 us  [local(): got = lax.all_to_all(piece, ('y', 'near'), 0, 0, tiled=True)]
    all_to_all x1, starting transfers between devices: 12.1 us -> 9.2 us  [local(): got = lax.all_to_all(piece, ('y', 'near'), 0, 0, tiled=True)]
    all_to_all x1, blocking collectives: 12.9 us -> 10.7 us  [local(): entering = lax.all_to_all(joint, ('y', 'near'), 0, 0, tiled=True)]
    all_to_all x1, blocking collectives: 13.7 us -> 14.9 us  [local(): powers = lax.all_to_all(power, 'head', 0, 0, tiled=True)]
where the time goes in v7:
time: 74.6 us; the launch traced here: 74.2 us
  blocking collectives  48.9 us (66%)
  Pallas kernels  9.23 us (12%)
  starting transfers between devices  9.2 us (12%)
  waiting for transfers between devices  5.5 us (7%)
  local copies, waits for them, and re-layouts  1.35 us (2%)
    all_gather x1, blocking collectives, local(): totals = lax.all_gather(total, 'far')  23.3 us
    all_to_all x1, blocking collectives, local(): powers = lax.all_to_all(power, 'head', 0, 0, tiled=True)  14.9 us
    all_to_all x1, blocking collectives, local(): entering = lax.all_to_all(joint, ('y', 'near'), 0, 0, tiled=True)  10.7 us
    all_to_all x1, starting transfers between devices, local(): got = lax.all_to_all(piece, ('y', 'near'), 0, 0, tiled=True)  9.2 us
    all_to_all x1, waiting for transfers between devices, local(): got = lax.all_to_all(piece, ('y', 'near'), 0, 0, tiled=True)  5.5 us
    pallas_call x1, Pallas kernels, local(): call(functools.partial(inner_kernel, heads, blocks), (((rows, width), f32...  4.41 us
    pallas_call x1, Pallas kernels, local(): call(functools.partial(summary_kernel, heads, blocks), (((OWNERS, PIECE_R...  3.01 us
  transfers between devices with their start and end apart: 1, of which 1 were waited for; matrix products, arithmetic and copies ran while one was open for 0% of the time, Pallas kernels for 6%

profile of v7, /device:TPU:1, one launch (start us, length us, event | category | flops | bytes accessed | tf_op | source)
XLA Modules:
  0.0 74.2 jit_solution(8451571013379561187)
XLA Ops:
  0.0 3.0 %shard_map.82 = f32[16,40,128]{2,1,0:T(8,128)} custom-call(f32[4]{0:T(128)} %rate_hbm.3, s32[4,1024]{1,0:T(4,128)} %codes_hbm.3, bf16[1024,128]{1,0:T(8,128)(2,1)} %write_hbm.3, bf16[1024,512]{1,0:T(8,128)(2,1)} %x_hbm.3), custom_call_target="tpu_custom_call" | custom-call | flops 268435456 | bytes 3145728 | tf_op jit(solution)/shard_map/pallas_call | solution.py:306
  3.0 9.2 %all-to-all-start = ((f32[16,40,128]{2,1,0:T(8,128)}), f32[16,40,128]{2,1,0:T(8,128)S(1)}, u32[]{:S(2)}, u32[]{:S(2)}) async-start(f32[16,40,128]{2,1,0:T(8,128)} %shard_map.82), calls=%async_computation | async-start | bytes 655360 | tf_op jit(solution)/shard_map/all_to_all | solution.py:321
  12.2 4.4 %shard_map.83 = (f32[1024,512]{1,0:T(8,128)S(1)}, f32[1024,512]{1,0:T(8,128)S(1)}, f32[4,512]{1,0:T(4,128)S(1)}, f32[3,128,512]{2,1,0:T(8,128)S(1)}) custom-call(f32[4]{0:T(128)} %rate_hbm.3, f32[4]{0:T(128)} %skip_hbm.1, s32[4,1024]{1,0:T(4,128)} %codes_hbm.3, bf16[1024,128]{1,0:T(8,128)(2,1)} %write_hbm.3, bf16[1024,128]{1,0:T(8,128)(2,1)} %read_ref.1, ...), custom_call_target="tpu_custom_call" | custom-call | flops 1073741824 | bytes 7340032 | tf_op jit(solution)/shard_map/pallas_call | solution.py:322
  16.7 0.0 copy-start
  16.7 1.3 %copy-done = f32[1024,512]{1,0:T(8,128)} copy-done((f32[1024,512]{1,0:T(8,128)}, f32[1024,512]{1,0:T(8,128)S(1)}, u32[]{:S(2)}) %copy-start) | copy-done | bytes 2097176
  18.0 5.5 %all-to-all-done.got_ref = f32[16,40,128]{2,1,0:T(8,128)S(1)} async-done(((f32[16,40,128]{2,1,0:T(8,128)}), f32[16,40,128]{2,1,0:T(8,128)S(1)}, u32[]{:S(2)}, u32[]{:S(2)}) %all-to-all-start) | async-done | bytes 327712 | tf_op jit(solution)/shard_map/all_to_all | solution.py:321
  23.5 23.3 %all-gather = f32[544,128]{1,0:T(8,128)S(1)} all-gather(f32[136,128]{1,0:T(8,128)S(1)} %get-tuple-element.24), channel_id=2, replica_groups=mesh['y'=4,'far'=4,'near'=4,'head'=8] {'far'}, dimensions={0}, use_global_device_ids=true | all-gather | bytes 348160 | tf_op jit(solution)/shard_map/all_gather | solution.py:349
  46.9 0.0 copy-start.1
  46.9 0.0 copy-start.2
  46.9 0.1 shard_map.85
  46.9 10.7 %all_to_all.15.entering_ref = f32[16,32,128]{2,1,0:T(8,128)S(1)} all-to-all(f32[16,32,128]{2,1,0:T(8,128)S(1)} %shard_map.85), channel_id=1, replica_groups=mesh['y'=4,'far'=4,'near'=4,'head'=8] {'y','near'}, dimensions={0} | all-to-all | bytes 524288 | tf_op jit(solution)/shard_map/all_to_all | solution.py:353
  57.6 0.0 copy-done.1
  57.7 0.0 copy-done.2
  57.7 0.0 copy-start.3
  57.7 0.6 shard_map.86
  58.2 14.9 %all_to_all.16.power_ref = f32[8,8,128]{2,1,0:T(8,128)S(1)} all-to-all(f32[8,8,128]{2,1,0:T(8,128)S(1)} %get-tuple-element.31), channel_id=1, replica_groups=mesh['y'=4,'far'=4,'near'=4,'head'=8] {'head'}, dimensions={0} | all-to-all | bytes 65536 | tf_op jit(solution)/shard_map/all_to_all | solution.py:362
  73.1 0.0 copy-done.3
  73.1 1.2 %shard_map.87 = bf16[1024,512]{1,0:T(8,128)(2,1)} custom-call(f32[8,8,128]{2,1,0:T(8,128)S(1)} %all_to_all.16.power_ref, f32[1,512]{1,0:T(1,128)S(1)} %bitcast.3, f32[1024,512]{1,0:T(8,128)S(1)} %get-tuple-element.32.gated_ref), custom_call_target="tpu_custom_call" | custom-call | flops 1048576 | bytes 3145728 | tf_op jit(solution)/shard_map/pallas_call | solution.py:363
  (1 shorter events, 0.0 us)
Async XLA Ops:
  3.0 20.5 %all-to-all-start = ((f32[16,40,128]{2,1,0:T(8,128)}), f32[16,40,128]{2,1,0:T(8,128)S(1)}, u32[]{:S(2)}, u32[]{:S(2)}) async-start(f32[16,40,128]{2,1,0:T(8,128)} %shard_map.82), calls=%async_computation | async-start | bytes 655360 | tf_op jit(solution)/shard_map/all_to_all | solution.py:321
  16.7 1.3 %copy-start = (f32[1024,512]{1,0:T(8,128)}, f32[1024,512]{1,0:T(8,128)S(1)}, u32[]{:S(2)}) copy-start(f32[1024,512]{1,0:T(8,128)S(1)} %get-tuple-element.30.factor_ref) | copy-start | bytes 6291460
  46.9 10.8 %copy-start.1 = (f32[1024,512]{1,0:T(8,128)S(1)}, f32[1024,512]{1,0:T(8,128)}, u32[]{:S(2)}) copy-start(f32[1024,512]{1,0:T(8,128)} %copy-done) | copy-start | bytes 6291460
  46.9 10.8 %copy-start.2 = (bf16[1024,128]{1,0:T(8,128)(2,1)S(1)}, bf16[1024,128]{1,0:T(8,128)(2,1)}, u32[]{:S(2)}) copy-start(bf16[1024,128]{1,0:T(8,128)(2,1)} %read_ref.1) | copy-start | bytes 786436
  57.7 15.4 %copy-start.3 = (f32[512]{0:T(512)S(1)}, f32[512]{0:T(512)}, u32[]{:S(2)}) copy-start(f32[512]{0:T(512)} %param.15) | copy-start | bytes 6148

commit v8 on v7

--- a/solution.py
+++ b/solution.py
@@ -88,14 +88,16 @@
     codes_hbm,
     write_hbm,
     x_hbm,
-    piece_ref,
+    piece_hbm,
     rate_ref,
     codes_ref,
     write_ref,
     x_ref,
+    piece_ref,
     sem,
+    out_sem,
 ):
-    pairs = ((rate_hbm, rate_ref), (codes_hbm, codes_ref), (write_hbm, write_ref), (x_hbm, x_ref))
+    pairs = ((rate_hbm, rate_ref), (codes_hbm, codes_ref), (x_hbm, x_ref), (write_hbm, write_ref))
     copies = [pltpu.make_async_copy(a, b, sem.at[i]) for i, (a, b) in enumerate(pairs)]
     for copy in copies:
         copy.start()
@@ -117,11 +119,17 @@
         added = matmul(write_ref[rows, :], weighted_inputs(tail, x_ref, rows, k, heads), TN)
         state = head_lanes(block_decay, k * heads, heads) * state + added if k else added
     quarters = STATE // PIECE
+    sent = []
     for h in range(heads):
         decay = jnp.broadcast_to(section_decay[:, h : h + 1], (PIECE_ROWS - PIECE, LANES))
         for q in range(quarters):
             piece_ref[h * quarters + q, :PIECE, :] = state[q * PIECE : (q + 1) * PIECE, h * LANES : (h + 1) * LANES]
             piece_ref[h * quarters + q, PIECE:, :] = decay
+        own = pl.ds(h * quarters, quarters)
+        sent.append(pltpu.make_async_copy(piece_ref.at[own], piece_hbm.at[own], out_sem.at[h]))
+        sent[-1].start()
+    for copy in sent:
+        copy.wait()
 
 
 def inner_kernel(
@@ -264,10 +272,11 @@
 def norm_kernel(heads, power_ref, gain_ref, gated_ref, out_hbm, out_ref, out_sem):
     power = sum(power_ref[j] for j in range(HEAD)) * (1.0 / CHANNELS)
     scale = lax.rsqrt(power + EPS)
+    columns = [jnp.broadcast_to(scale[r : r + 1, :], (LANES, LANES)).T for r in range(scale.shape[0])]
     copies = []
     for r in range(scale.shape[0]):
         rows = pl.ds(r * LANES, LANES)
-        column = jnp.broadcast_to(scale[r : r + 1, :], (LANES, LANES)).T
+        column = columns[r]
         for h in range(heads):
             lanes = slice(h * LANES, (h + 1) * LANES)
             out_ref[rows, lanes] = (gated_ref[rows, lanes] * column * gain_ref[:, lanes]).astype(jnp.bfloat16)
@@ -315,8 +324,11 @@
             pltpu.VMEM(decay_codes.shape, jnp.int32),
             pltpu.VMEM(write_proj.shape, bf16),
             pltpu.VMEM(ssm_input.shape, bf16),
+            pltpu.VMEM((OWNERS, PIECE_ROWS, LANES), f32),
             pltpu.SemaphoreType.DMA((4,)),
+            pltpu.SemaphoreType.DMA((heads,)),
         ),
+        HBM,
     )(*in_hbm(decay_rate, decay_codes, write_proj, ssm_input))
     got = lax.all_to_all(piece, ("y", "near"), 0, 0, tiled=True)
     base, factor, lead, own = call(

time: 74.6 us -> 74.5 us (level)
  no operation moved by 1% of the time
where the time goes in v8:
time: 74.5 us; the launch traced here: 74.2 us
  blocking collectives  48.9 us (66%)
  Pallas kernels  9.2 us (12%)
  starting transfers between devices  9.2 us (12%)
  waiting for transfers between devices  5.5 us (7%)
  local copies, waits for them, and re-layouts  1.35 us (2%)
    all_gather x1, blocking collectives, local(): totals = lax.all_gather(total, 'far')  23.3 us
    all_to_all x1, blocking collectives, local(): powers = lax.all_to_all(power, 'head', 0, 0, tiled=True)  14.9 us
    all_to_all x1, blocking collectives, local(): entering = lax.all_to_all(joint, ('y', 'near'), 0, 0, tiled=True)  10.7 us
    all_to_all x1, starting transfers between devices, local(): got = lax.all_to_all(piece, ('y', 'near'), 0, 0, tiled=True)  9.2 us
    all_to_all x1, waiting for transfers between devices, local(): got = lax.all_to_all(piece, ('y', 'near'), 0, 0, tiled=True)  5.5 us
    pallas_call x1, Pallas kernels, local(): call(functools.partial(inner_kernel, heads, blocks), (((rows, width), f32...  4.41 us
    pallas_call x1, Pallas kernels, local(): call(functools.partial(summary_kernel, heads, blocks), (((OWNERS, PIECE_R...  2.99 us
  transfers between devices with their start and end apart: 1, of which 1 were waited for; matrix products, arithmetic and copies ran while one was open for 0% of the time, Pallas kernels for 6%

profile of v8, /device:TPU:1, one launch (start us, length us, event | category | flops | bytes accessed | tf_op | source)
XLA Modules:
  0.0 74.2 jit_solution(7631155130895001778)
XLA Ops:
  0.0 3.0 %shard_map.82 = f32[16,40,128]{2,1,0:T(8,128)} custom-call(f32[4]{0:T(128)} %rate_hbm.3, s32[4,1024]{1,0:T(4,128)} %codes_hbm.3, bf16[1024,128]{1,0:T(8,128)(2,1)} %write_hbm.3, bf16[1024,512]{1,0:T(8,128)(2,1)} %x_hbm.3), custom_call_target="tpu_custom_call" | custom-call | flops 268435456 | bytes 3145728 | tf_op jit(solution)/shard_map/pallas_call | solution.py:315
  3.0 9.2 %all-to-all-start = ((f32[16,40,128]{2,1,0:T(8,128)}), f32[16,40,128]{2,1,0:T(8,128)S(1)}, u32[]{:S(2)}, u32[]{:S(2)}) async-start(f32[16,40,128]{2,1,0:T(8,128)} %shard_map.82), calls=%async_computation | async-start | bytes 655360 | tf_op jit(solution)/shard_map/all_to_all | solution.py:333
  12.2 4.4 %shard_map.83 = (f32[1024,512]{1,0:T(8,128)S(1)}, f32[1024,512]{1,0:T(8,128)S(1)}, f32[4,512]{1,0:T(4,128)S(1)}, f32[3,128,512]{2,1,0:T(8,128)S(1)}) custom-call(f32[4]{0:T(128)} %rate_hbm.3, f32[4]{0:T(128)} %skip_hbm.1, s32[4,1024]{1,0:T(4,128)} %codes_hbm.3, bf16[1024,128]{1,0:T(8,128)(2,1)} %write_hbm.3, bf16[1024,128]{1,0:T(8,128)(2,1)} %read_ref.1, ...), custom_call_target="tpu_custom_call" | custom-call | flops 1073741824 | bytes 7340032 | tf_op jit(solution)/shard_map/pallas_call | solution.py:334
  16.6 0.0 copy-start
  16.6 1.3 %copy-done = f32[1024,512]{1,0:T(8,128)} copy-done((f32[1024,512]{1,0:T(8,128)}, f32[1024,512]{1,0:T(8,128)S(1)}, u32[]{:S(2)}) %copy-start) | copy-done | bytes 2097176
  18.0 5.5 %all-to-all-done.got_ref = f32[16,40,128]{2,1,0:T(8,128)S(1)} async-done(((f32[16,40,128]{2,1,0:T(8,128)}), f32[16,40,128]{2,1,0:T(8,128)S(1)}, u32[]{:S(2)}, u32[]{:S(2)}) %all-to-all-start) | async-done | bytes 327712 | tf_op jit(solution)/shard_map/all_to_all | solution.py:333
  23.5 23.3 %all-gather = f32[544,128]{1,0:T(8,128)S(1)} all-gather(f32[136,128]{1,0:T(8,128)S(1)} %get-tuple-element.24), channel_id=2, replica_groups=mesh['y'=4,'far'=4,'near'=4,'head'=8] {'far'}, dimensions={0}, use_global_device_ids=true | all-gather | bytes 348160 | tf_op jit(solution)/shard_map/all_gather | solution.py:361
  46.8 0.0 copy-start.1
  46.8 0.0 copy-start.2
  46.8 0.1 shard_map.85
  46.9 10.7 %all_to_all.15.entering_ref = f32[16,32,128]{2,1,0:T(8,128)S(1)} all-to-all(f32[16,32,128]{2,1,0:T(8,128)S(1)} %shard_map.85), channel_id=1, replica_groups=mesh['y'=4,'far'=4,'near'=4,'head'=8] {'y','near'}, dimensions={0} | all-to-all | bytes 524288 | tf_op jit(solution)/shard_map/all_to_all | solution.py:365
  57.6 0.0 copy-done.1
  57.6 0.0 copy-done.2
  57.6 0.0 copy-start.3
  57.6 0.6 shard_map.86
  58.2 14.9 %all_to_all.16.power_ref = f32[8,8,128]{2,1,0:T(8,128)S(1)} all-to-all(f32[8,8,128]{2,1,0:T(8,128)S(1)} %get-tuple-element.31), channel_id=1, replica_groups=mesh['y'=4,'far'=4,'near'=4,'head'=8] {'head'}, dimensions={0} | all-to-all | bytes 65536 | tf_op jit(solution)/shard_map/all_to_all | solution.py:374
  73.0 0.0 copy-done.3
  73.0 1.2 %shard_map.87 = bf16[1024,512]{1,0:T(8,128)(2,1)} custom-call(f32[8,8,128]{2,1,0:T(8,128)S(1)} %all_to_all.16.power_ref, f32[1,512]{1,0:T(1,128)S(1)} %bitcast.3, f32[1024,512]{1,0:T(8,128)S(1)} %get-tuple-element.32.gated_ref), custom_call_target="tpu_custom_call" | custom-call | flops 1048576 | bytes 3145728 | tf_op jit(solution)/shard_map/pallas_call | solution.py:375
  (1 shorter events, 0.0 us)
Async XLA Ops:
  3.0 20.5 %all-to-all-start = ((f32[16,40,128]{2,1,0:T(8,128)}), f32[16,40,128]{2,1,0:T(8,128)S(1)}, u32[]{:S(2)}, u32[]{:S(2)}) async-start(f32[16,40,128]{2,1,0:T(8,128)} %shard_map.82), calls=%async_computation | async-start | bytes 655360 | tf_op jit(solution)/shard_map/all_to_all | solution.py:333
  16.6 1.3 %copy-start = (f32[1024,512]{1,0:T(8,128)}, f32[1024,512]{1,0:T(8,128)S(1)}, u32[]{:S(2)}) copy-start(f32[1024,512]{1,0:T(8,128)S(1)} %get-tuple-element.30.factor_ref) | copy-start | bytes 6291460
  46.8 10.8 %copy-start.1 = (f32[1024,512]{1,0:T(8,128)S(1)}, f32[1024,512]{1,0:T(8,128)}, u32[]{:S(2)}) copy-start(f32[1024,512]{1,0:T(8,128)} %copy-done) | copy-start | bytes 6291460
  46.8 10.8 %copy-start.2 = (bf16[1024,128]{1,0:T(8,128)(2,1)S(1)}, bf16[1024,128]{1,0:T(8,128)(2,1)}, u32[]{:S(2)}) copy-start(bf16[1024,128]{1,0:T(8,128)(2,1)} %read_ref.1) | copy-start | bytes 786436
  57.6 15.4 %copy-start.3 = (f32[512]{0:T(512)S(1)}, f32[512]{0:T(512)}, u32[]{:S(2)}) copy-start(f32[512]{0:T(512)} %param.15) | copy-start | bytes 6148

commit v9 on v7

--- a/solution.py
+++ b/solution.py
@@ -19,7 +19,7 @@
 STATE = 128
 OWNERS = Y * NEAR
 PIECE = 32
-PIECE_ROWS = 40
+PIECE_ROWS = 33
 TOTAL_ROWS = Y * PIECE + 8
 MIB = 1 << 20
 NT = (((1,), (1,)), ((), ()))

time: 74.6 us -> 74.6 us (level)
  no operation moved by 1% of the time
where the time goes in v9:
time: 74.6 us; the launch traced here: 74.2 us
  blocking collectives  48.9 us (66%)
  Pallas kernels  9.22 us (12%)
  starting transfers between devices  9.19 us (12%)
  waiting for transfers between devices  5.5 us (7%)
  local copies, waits for them, and re-layouts  1.35 us (2%)
    all_gather x1, blocking collectives, local(): totals = lax.all_gather(total, 'far')  22.7 us
    all_to_all x1, blocking collectives, local(): powers = lax.all_to_all(power, 'head', 0, 0, tiled=True)  14.9 us
    all_to_all x1, blocking collectives, local(): entering = lax.all_to_all(joint, ('y', 'near'), 0, 0, tiled=True)  11.3 us
    all_to_all x1, starting transfers between devices, local(): got = lax.all_to_all(piece, ('y', 'near'), 0, 0, tiled=True)  9.19 us
    all_to_all x1, waiting for transfers between devices, local(): got = lax.all_to_all(piece, ('y', 'near'), 0, 0, tiled=True)  5.5 us
    pallas_call x1, Pallas kernels, local(): call(functools.partial(inner_kernel, heads, blocks), (((rows, width), f32...  4.41 us
    pallas_call x1, Pallas kernels, local(): call(functools.partial(summary_kernel, heads, blocks), (((OWNERS, PIECE_R...  3.01 us
  transfers between devices with their start and end apart: 1, of which 1 were waited for; matrix products, arithmetic and copies ran while one was open for 0% of the time, Pallas kernels for 6%

profile of v9, /device:TPU:1, one launch (start us, length us, event | category | flops | bytes accessed | tf_op | source)
XLA Modules:
  0.0 74.2 jit_solution(8877792403402630722)
XLA Ops:
  0.0 3.0 %shard_map.82 = f32[16,33,128]{2,1,0:T(8,128)} custom-call(f32[4]{0:T(128)} %rate_hbm.3, s32[4,1024]{1,0:T(4,128)} %codes_hbm.3, bf16[1024,128]{1,0:T(8,128)(2,1)} %write_hbm.3, bf16[1024,512]{1,0:T(8,128)(2,1)} %x_hbm.3), custom_call_target="tpu_custom_call" | custom-call | flops 268435456 | bytes 3145728 | tf_op jit(solution)/shard_map/pallas_call | solution.py:306
  3.0 9.2 %all-to-all-start = ((f32[16,33,128]{2,1,0:T(8,128)}), f32[16,33,128]{2,1,0:T(8,128)S(1)}, u32[]{:S(2)}, u32[]{:S(2)}) async-start(f32[16,33,128]{2,1,0:T(8,128)} %shard_map.82), calls=%async_computation | async-start | bytes 655360 | tf_op jit(solution)/shard_map/all_to_all | solution.py:321
  12.2 4.4 %shard_map.83 = (f32[1024,512]{1,0:T(8,128)S(1)}, f32[1024,512]{1,0:T(8,128)S(1)}, f32[4,512]{1,0:T(4,128)S(1)}, f32[3,128,512]{2,1,0:T(8,128)S(1)}) custom-call(f32[4]{0:T(128)} %rate_hbm.3, f32[4]{0:T(128)} %skip_hbm.1, s32[4,1024]{1,0:T(4,128)} %codes_hbm.3, bf16[1024,128]{1,0:T(8,128)(2,1)} %write_hbm.3, bf16[1024,128]{1,0:T(8,128)(2,1)} %read_ref.1, ...), custom_call_target="tpu_custom_call" | custom-call | flops 1073741824 | bytes 7340032 | tf_op jit(solution)/shard_map/pallas_call | solution.py:322
  16.6 0.0 copy-start
  16.7 1.3 %copy-done = f32[1024,512]{1,0:T(8,128)} copy-done((f32[1024,512]{1,0:T(8,128)}, f32[1024,512]{1,0:T(8,128)S(1)}, u32[]{:S(2)}) %copy-start) | copy-done | bytes 2097176
  18.0 5.5 %all-to-all-done.got_ref = f32[16,33,128]{2,1,0:T(8,128)S(1)} async-done(((f32[16,33,128]{2,1,0:T(8,128)}), f32[16,33,128]{2,1,0:T(8,128)S(1)}, u32[]{:S(2)}, u32[]{:S(2)}) %all-to-all-start) | async-done | bytes 270368 | tf_op jit(solution)/shard_map/all_to_all | solution.py:321
  23.5 22.7 %all-gather = f32[544,128]{1,0:T(8,128)S(1)} all-gather(f32[136,128]{1,0:T(8,128)S(1)} %get-tuple-element.24), channel_id=2, replica_groups=mesh['y'=4,'far'=4,'near'=4,'head'=8] {'far'}, dimensions={0}, use_global_device_ids=true | all-gather | bytes 348160 | tf_op jit(solution)/shard_map/all_gather | solution.py:349
  46.2 0.0 copy-start.1
  46.2 0.0 copy-start.2
  46.2 0.1 shard_map.85
  46.2 11.3 %all_to_all.15.entering_ref = f32[16,32,128]{2,1,0:T(8,128)S(1)} all-to-all(f32[16,32,128]{2,1,0:T(8,128)S(1)} %shard_map.85), channel_id=1, replica_groups=mesh['y'=4,'far'=4,'near'=4,'head'=8] {'y','near'}, dimensions={0} | all-to-all | bytes 524288 | tf_op jit(solution)/shard_map/all_to_all | solution.py:353
  57.6 0.0 copy-done.1
  57.6 0.0 copy-done.2
  57.6 0.0 copy-start.3
  57.6 0.6 shard_map.86
  58.2 14.9 %all_to_all.16.power_ref = f32[8,8,128]{2,1,0:T(8,128)S(1)} all-to-all(f32[8,8,128]{2,1,0:T(8,128)S(1)} %get-tuple-element.31), channel_id=1, replica_groups=mesh['y'=4,'far'=4,'near'=4,'head'=8] {'head'}, dimensions={0} | all-to-all | bytes 65536 | tf_op jit(solution)/shard_map/all_to_all | solution.py:362
  73.1 0.0 copy-done.3
  73.1 1.2 %shard_map.87 = bf16[1024,512]{1,0:T(8,128)(2,1)} custom-call(f32[8,8,128]{2,1,0:T(8,128)S(1)} %all_to_all.16.power_ref, f32[1,512]{1,0:T(1,128)S(1)} %bitcast.3, f32[1024,512]{1,0:T(8,128)S(1)} %get-tuple-element.32.gated_ref), custom_call_target="tpu_custom_call" | custom-call | flops 1048576 | bytes 3145728 | tf_op jit(solution)/shard_map/pallas_call | solution.py:363
  (1 shorter events, 0.0 us)
Async XLA Ops:
  3.0 20.5 %all-to-all-start = ((f32[16,33,128]{2,1,0:T(8,128)}), f32[16,33,128]{2,1,0:T(8,128)S(1)}, u32[]{:S(2)}, u32[]{:S(2)}) async-start(f32[16,33,128]{2,1,0:T(8,128)} %shard_map.82), calls=%async_computation | async-start | bytes 655360 | tf_op jit(solution)/shard_map/all_to_all | solution.py:321
  16.6 1.3 %copy-start = (f32[1024,512]{1,0:T(8,128)}, f32[1024,512]{1,0:T(8,128)S(1)}, u32[]{:S(2)}) copy-start(f32[1024,512]{1,0:T(8,128)S(1)} %get-tuple-element.30.factor_ref) | copy-start | bytes 6291460
  46.2 11.4 %copy-start.1 = (f32[1024,512]{1,0:T(8,128)S(1)}, f32[1024,512]{1,0:T(8,128)}, u32[]{:S(2)}) copy-start(f32[1024,512]{1,0:T(8,128)} %copy-done) | copy-start | bytes 6291460
  46.2 11.4 %copy-start.2 = (bf16[1024,128]{1,0:T(8,128)(2,1)S(1)}, bf16[1024,128]{1,0:T(8,128)(2,1)}, u32[]{:S(2)}) copy-start(bf16[1024,128]{1,0:T(8,128)(2,1)} %read_ref.1) | copy-start | bytes 786436
  57.6 15.5 %copy-start.3 = (f32[512]{0:T(512)S(1)}, f32[512]{0:T(512)}, u32[]{:S(2)}) copy-start(f32[512]{0:T(512)} %param.15) | copy-start | bytes 6148
